TPU v7x, 512 devices: a whole 4x4x16 slice. The times are simulated.
512 devices in a mesh: samp: 32 (over y, x, core), kmer: 16 (over z).
Axes of the slice: x: 4, y: 4, z: 16, core: 2. Of those that a mesh axis runs over, the one named last changes fastest.
Arguments:
- tile_rows: int32 [32, 16, 32], P('samp', 'kmer'), may hold values from 0 to 3, as said below
- tile_cols: int32 [32, 16, 32], P('samp', 'kmer'), may hold values from 0 to 31
- tile_count: int32 [32, 16], P('samp', 'kmer'), may hold values from 4 to 32, as said below
- tile_values: bfloat16 [32, 16, 32, 128, 128], P('samp', 'kmer'), may hold values from 0.049804688 to 20
- w_init: float32 [16384, 64], P(('samp', 'kmer')), may hold values from 0.1 to 30, as said below
- h_init: float32 [64, 65536], P(None, ('kmer', 'samp')), may hold values from 0.1 to 30, as said below
Outputs:
- w_final: float32 [16384, 64], P(('samp', 'kmer'))
- h_final: float32 [64, 65536], P(None, ('kmer', 'samp'))
Inputs may be any that keep to these rules, and one draw needn't show every extreme that they name: Within a device all 32 slots hold distinct (tile_rows, tile_cols) pairs. `tile_count`: some device has all 32 slots live in every draw. `w_init`: Positive. `h_init`: Positive.
All inputs are finite; a program needn't handle non-finite values.
Results may differ from a plain program's by a relative error of at most 0.00051.
Values may be sent and summed in bfloat16 or wider, within the bound.
No kernel may reach another device: no remote copies, remote signals or barrier semaphores. Data moves between devices by JAX's collectives and lax.ppermute only.
A program may use at most 64 MiB of HBM per device.

v0:
```python
import jax
import jax.numpy as jnp
from jax import lax
from jax.sharding import PartitionSpec as P

ROW_TILES = 4
COL_TILES = 32
ITERS = 2


def panel_of(h_state):
    return lax.all_gather(h_state.astype(jnp.bfloat16), "samp", axis=1, tiled=True)


def update_h(h_state, numerator, col_total):
    summed = lax.psum_scatter(numerator, "samp", scatter_dimension=1, tiled=True)
    return h_state * summed / col_total[:, None]


def column_total(w_half):
    return lax.psum(jnp.sum(w_half.astype(jnp.float32), axis=0), ("samp", "kmer"))


def row_total(h_half_own):
    return lax.psum(jnp.sum(h_half_own.astype(jnp.float32), axis=1), ("samp", "kmer"))


def tile_ratio(w_tiles, h_panel, col_index, values, live_slots, rank_size, tile_size):
    h_tiles = jnp.take(h_panel.reshape(rank_size, -1, tile_size), col_index, axis=1)
    estimate = jnp.einsum("gik,kgj->gij", w_tiles, h_tiles, preferred_element_type=jnp.float32)
    ratio = jnp.where(live_slots[:, None, None], values.astype(jnp.float32) / estimate, 0.0)
    return (h_tiles, ratio.astype(jnp.bfloat16))


def body(tile_rows, tile_cols, tile_count, tile_values, w_init, h_init):
    tile_size = tile_values.shape[-1]
    rank_size = w_init.shape[1]
    values = tile_values.reshape(-1, tile_size, tile_size)
    row_index = tile_rows.reshape(-1)
    col_index = tile_cols.reshape(-1)
    live_slots = jnp.arange(row_index.shape[0], dtype=jnp.int32) < tile_count.reshape(())
    col_hot = (col_index[:, None] == jnp.arange(COL_TILES, dtype=jnp.int32)[None, :]).astype(
        jnp.float32
    )
    row_hot = (row_index[:, None] == jnp.arange(ROW_TILES, dtype=jnp.int32)[None, :]).astype(
        jnp.float32
    )
    w_full = w_init
    h_state = h_init
    h_panel = panel_of(h_state)
    for sweep_index in range(ITERS):
        w_half = w_full.astype(jnp.bfloat16)
        w_panel = lax.all_gather(w_half, "kmer", axis=0, tiled=True)
        w_tiles = jnp.take(w_panel.reshape(ROW_TILES, tile_size, rank_size), row_index, axis=0)
        col_total = column_total(w_half)
        h_tiles, ratio = tile_ratio(
            w_tiles, h_panel, col_index, values, live_slots, rank_size, tile_size
        )
        contribution = jnp.einsum(
            "gik,gij->gkj", w_tiles, ratio, preferred_element_type=jnp.float32
        )
        numerator = jnp.einsum(
            "gc,gkj->kcj", col_hot, contribution, precision=lax.Precision.HIGHEST
        )
        h_state = update_h(h_state, numerator.reshape(rank_size, -1), col_total)
        h_panel = panel_of(h_state)
        h_half_own = h_state.astype(jnp.bfloat16)
        h_sum_rows = row_total(h_half_own)
        h_tiles, ratio = tile_ratio(
            w_tiles, h_panel, col_index, values, live_slots, rank_size, tile_size
        )
        contribution = jnp.einsum(
            "gij,kgj->gik", ratio, h_tiles, preferred_element_type=jnp.float32
        )
        numerator = jnp.einsum(
            "gr,gik->rik", row_hot, contribution, precision=lax.Precision.HIGHEST
        )
        numerator = lax.psum_scatter(
            numerator.reshape(-1, rank_size), "kmer", scatter_dimension=0, tiled=True
        )
        w_full = w_full * numerator / h_sum_rows[None, :]
    return (w_full, h_state)


def solution(mesh):
    in_specs = (
        P("samp", "kmer", None),
        P("samp", "kmer", None),
        P("samp", "kmer"),
        P("samp", "kmer", None, None, None),
        P(("samp", "kmer"), None),
        P(None, ("kmer", "samp")),
    )
    out_specs = (P(("samp", "kmer"), None), P(None, ("kmer", "samp")))
    return jax.shard_map(body, mesh=mesh, in_specs=in_specs, out_specs=out_specs, check_vma=False)
```

profile of v0, /device:TPU:1, one launch (start us, length us, event | category | flops | bytes accessed | tf_op | source)
XLA Modules:
  0.0 579.9 jit_solution(11328605241868232257)
XLA Ops:
  7.2 0.7 compare_select_fusion.1
  7.9 0.7 compare_select_fusion
  8.5 0.7 compare_and_fusion
  9.9 0.7 convert_reduce_fusion.3
  10.6 0.8 convert_element_type.55
  11.4 29.9 %all_gather.15 = bf16[512,64]{1,0:T(8,128)(2,1)S(1)} all-gather(bf16[32,64]{1,0:T(8,128)(2,1)S(1)} %get-tuple-element.12), channel_id=1, replica_groups=mesh['samp'=32,'kmer'=16] {'kmer'}, dimensions={0}, use_global_device_ids=true | all-gather | bytes 69632 | tf_op jit(solution)/shard_map/all_gather | solution.py:53
  41.4 32.8 %all_gather.16 = bf16[64,4096]{1,0:T(8,128)(2,1)S(1)} all-gather(bf16[64,128]{1,0:T(8,128)(2,1)S(1)} %convert_element_type.55), channel_id=1, replica_groups=mesh['samp'=32,'kmer'=16] {'samp'}, dimensions={1}, use_global_device_ids=true | all-gather | bytes 540672 | tf_op jit(solution)/shard_map/all_gather | solution.py:12
  74.3 0.7 gather_fusion
  76.2 1.0 fusion.9
  77.2 1.3 fusion.22
  78.4 1.6 copy.68
  80.1 99.4 %psum.28 = f32[64]{0:T(128)S(1)} all-reduce(f32[64]{0:T(128)S(1)} %get-tuple-element.11), channel_id=1, replica_groups=mesh['samp'=32,'kmer'=16] {'samp','kmer'}, use_global_device_ids=true, to_apply=%region_2.0 | all-reduce | flops 64 | bytes 512 | tf_op jit(solution)/shard_map/psum | solution.py:21
  179.5 0.9 convert_reduce_fusion.1
  180.4 24.8 %all_gather.17 = bf16[64,4096]{1,0:T(8,128)(2,1)S(1)} all-gather(bf16[64,128]{1,0:T(8,128)(2,1)S(1)} %get-tuple-element.10), channel_id=1, replica_groups=mesh['samp'=32,'kmer'=16] {'samp'}, dimensions={1}, use_global_device_ids=true | all-gather | bytes 540672 | tf_op jit(solution)/shard_map/all_gather | solution.py:12
  206.1 1.3 fusion.11
  207.4 1.0 fusion.20
  208.4 0.8 copy.45
  209.3 100.7 %psum.29 = f32[64]{0:T(128)S(1)} all-reduce(f32[64]{0:T(128)S(1)} %get-tuple-element.9), channel_id=1, replica_groups=mesh['samp'=32,'kmer'=16] {'samp','kmer'}, use_global_device_ids=true, to_apply=%region_5.8 | all-reduce | flops 64 | bytes 512 | tf_op jit(solution)/shard_map/psum | solution.py:25
  310.0 0.7 convert_reduce_fusion.2
  310.8 20.3 %all_gather.18 = bf16[512,64]{1,0:T(8,128)(2,1)S(1)} all-gather(bf16[32,64]{1,0:T(8,128)(2,1)S(1)} %get-tuple-element.8), channel_id=1, replica_groups=mesh['samp'=32,'kmer'=16] {'kmer'}, dimensions={0}, use_global_device_ids=true | all-gather | bytes 69632 | tf_op jit(solution)/shard_map/all_gather | solution.py:53
  331.8 1.0 fusion.8
  332.8 1.3 fusion.18
  334.1 1.6 copy.67
  335.8 105.2 %psum.30 = f32[64]{0:T(128)S(1)} all-reduce(f32[64]{0:T(128)S(1)} %get-tuple-element.7), channel_id=1, replica_groups=mesh['samp'=32,'kmer'=16] {'samp','kmer'}, use_global_device_ids=true, to_apply=%region_8.11 | all-reduce | flops 64 | bytes 512 | tf_op jit(solution)/shard_map/psum | solution.py:21
  441.0 1.6 convert_reduce_fusion
  442.5 25.0 %all_gather.19 = bf16[64,4096]{1,0:T(8,128)(2,1)S(1)} all-gather(bf16[64,128]{1,0:T(8,128)(2,1)S(1)} %get-tuple-element.5), channel_id=1, replica_groups=mesh['samp'=32,'kmer'=16] {'samp'}, dimensions={1}, use_global_device_ids=true | all-gather | bytes 540672 | tf_op jit(solution)/shard_map/all_gather | solution.py:12
  467.7 0.7 gather_fusion.4
  468.3 1.3 fusion.10
  469.6 1.1 fusion.16
  470.7 0.8 copy.48
  471.5 100.5 %psum.31 = f32[64]{0:T(128)S(1)} all-reduce(f32[64]{0:T(128)S(1)} %get-tuple-element.4), channel_id=1, replica_groups=mesh['samp'=32,'kmer'=16] {'samp','kmer'}, use_global_device_ids=true, to_apply=%region_11.14 | all-reduce | flops 64 | bytes 512 | tf_op jit(solution)/shard_map/psum | solution.py:25
  572.0 1.3 multiply_divide_fusion.2
  (37 shorter events, 3.4 us)
Async XLA Ops:
  7.2 172.3 %reduce-scatter.5.cloned.1.call-start = ((), (), s32[]{:S(2)}) async-start(), calls=%async_computation.4 | async-start | bytes 1081344 | tf_op jit(solution)/shard_map/reduce_scatter | solution.py:16
  74.9 1.2 copy-start.6
  76.2 1.0 copy-start.4
  80.0 99.4 %copy-start = (f32[64,128]{1,0:T(8,128)S(1)}, f32[64,128]{1,0:T(8,128)}, u32[]{:S(2)}) copy-start(f32[64,128]{1,0:T(8,128)} %param.15) | copy-start | bytes 98308
  80.1 229.9 %reduce-scatter.7.cloned.1.call-start = ((), (), s32[]{:S(2)}) async-start(), calls=%async_computation.5 | async-start | bytes 278528 | tf_op jit(solution)/shard_map/reduce_scatter | solution.py:78
  206.0 1.3 copy-start.5
  207.4 102.6 %copy-start.1 = (f32[32,64]{1,0:T(8,128)S(1)}, f32[32,64]{1,0:T(8,128)}, u32[]{:S(2)}) copy-start(f32[32,64]{1,0:T(8,128)} %param.14) | copy-start | bytes 24580
  209.3 231.7 %reduce-scatter.9.cloned.1.call-start = ((), (), s32[]{:S(2)}) async-start(), calls=%async_computation.6 | async-start | bytes 1081344 | tf_op jit(solution)/shard_map/reduce_scatter | solution.py:16
  335.7 105.3 %copy-start.2 = (f32[64,128]{1,0:T(8,128)S(1)}, f32[64,128]{1,0:T(8,128)}, u32[]{:S(2)}) copy-start(f32[64,128]{1,0:T(8,128)} %reduce-scatter.5.cloned.1.call-done) | copy-start | bytes 98308
  335.7 236.3 %reduce-scatter.11.cloned.1.call-start = ((), (), s32[]{:S(2)}) async-start(), calls=%async_computation.7 | async-start | bytes 278528 | tf_op jit(solution)/shard_map/reduce_scatter | solution.py:78
  469.6 102.4 %copy-start.3 = (f32[32,64]{1,0:T(8,128)S(1)}, f32[32,64]{1,0:T(8,128)}, u32[]{:S(2)}) copy-start(f32[32,64]{1,0:T(8,128)} %reduce-scatter.7.cloned.1.call-done) | copy-start | bytes 24580
Sparse Core Ops, SparseCore 0:
  80.2 92.3 reduce-scatter.4
  209.4 50.8 reduce-scatter.6
  335.8 99.0 reduce-scatter.8
  471.7 51.3 reduce-scatter.10
where the time goes:
time: 581 us; the launch traced here: 580 us
  blocking collectives  538 us (93%)
  between operations  14.6 us (3%)
  local copies, waits for them, and re-layouts  9.32 us (2%)
  matrix products  9.24 us (2%)
  other arithmetic  8.09 us (1%)
    psum x2, blocking collectives, column_total(): lax.psum(jnp.sum(w_half.astype(jnp.float32), axis=0), ('samp', 'kmer'))  205 us
    psum x2, blocking collectives, row_total(): lax.psum(jnp.sum(h_half_own.astype(jnp.float32), axis=1), ('samp', 'kmer'))  201 us
    all_gather x3, blocking collectives, panel_of(): lax.all_gather(h_state.astype(jnp.bfloat16), 'samp', axis=1, tiled=True)  82.6 us
    all_gather x2, blocking collectives, body(): w_panel = lax.all_gather(w_half, 'kmer', axis=0, tiled=True)  50.1 us
  transfers between devices with their start and end apart: 4, of which 0 were waited for; matrix products, arithmetic and copies ran while one was open for 0% of the time, Pallas kernels for 0%

commit v1 on v0

v1 whole, which is shorter than its diff:
```python
import jax
import jax.numpy as jnp
from jax import lax
from jax.sharding import PartitionSpec as P

ROW_TILES = 4
COL_TILES = 32
ITERS = 2
N_SAMP = 32
N_KMER = 16


def spread(x, axis_name, size):
    return lax.all_to_all(jnp.broadcast_to(x[None], (size,) + x.shape), axis_name, 0, 0)


def tile_ratio(w_tiles, h_tiles, values, live_slots):
    estimate = jnp.einsum("gik,gkj->gij", w_tiles, h_tiles, preferred_element_type=jnp.float32)
    ratio = jnp.where(live_slots[:, None, None], values.astype(jnp.float32) / estimate, 0.0)
    return ratio.astype(jnp.bfloat16)


def body(tile_rows, tile_cols, tile_count, tile_values, w_init, h_init):
    tile_size = tile_values.shape[-1]
    rank_size = w_init.shape[1]
    values = tile_values.reshape(-1, tile_size, tile_size)
    row_index = tile_rows.reshape(-1)
    col_index = tile_cols.reshape(-1)
    live_slots = jnp.arange(row_index.shape[0], dtype=jnp.int32) < tile_count.reshape(())
    col_hot = (col_index[:, None] == jnp.arange(COL_TILES, dtype=jnp.int32)[None, :]).astype(
        jnp.float32
    )
    row_hot = (row_index[:, None] == jnp.arange(ROW_TILES, dtype=jnp.int32)[None, :]).astype(
        jnp.float32
    )
    w_own = w_init
    h_own = h_init
    h_panel = spread(h_own.astype(jnp.bfloat16), "samp", N_SAMP)
    for sweep_index in range(ITERS):
        w_panel = spread(w_own.astype(jnp.bfloat16), "kmer", N_KMER)
        w_panel = w_panel.reshape(ROW_TILES, tile_size, rank_size)
        w_tiles = jnp.take(w_panel, row_index, axis=0)
        col_part = jnp.sum(w_panel.astype(jnp.float32), axis=(0, 1))
        h_tiles = jnp.take(h_panel, col_index, axis=0)
        ratio = tile_ratio(w_tiles, h_tiles, values, live_slots)
        contribution = jnp.einsum(
            "gik,gij->gkj", w_tiles, ratio, preferred_element_type=jnp.float32
        )
        numerator = jnp.einsum(
            "gc,gkj->ckj", col_hot, contribution, precision=lax.Precision.HIGHEST
        )
        col_row = jnp.pad(col_part, (0, tile_size - rank_size))
        col_rows = jnp.broadcast_to(col_row[None, None, :], (COL_TILES, 8, tile_size))
        parts = lax.all_to_all(jnp.concatenate([numerator, col_rows], axis=1), "samp", 0, 0)
        summed = jnp.sum(parts, axis=0)
        col_total = summed[rank_size, :rank_size]
        h_own = h_own * summed[:rank_size] / col_total[:, None]
        h_panel = spread(h_own.astype(jnp.bfloat16), "samp", N_SAMP)
        row_part = jnp.sum(h_panel.astype(jnp.float32), axis=(0, 2))
        h_tiles = jnp.take(h_panel, col_index, axis=0)
        ratio = tile_ratio(w_tiles, h_tiles, values, live_slots)
        contribution = jnp.einsum(
            "gij,gkj->gik", ratio, h_tiles, preferred_element_type=jnp.float32
        )
        numerator = jnp.einsum(
            "gr,gik->rik", row_hot, contribution, precision=lax.Precision.HIGHEST
        )
        numerator = numerator.reshape(N_KMER, -1, rank_size)
        row_rows = jnp.broadcast_to(row_part[None, None, :], (N_KMER, 8, rank_size))
        parts = lax.all_to_all(jnp.concatenate([numerator, row_rows], axis=1), "kmer", 0, 0)
        summed = jnp.sum(parts, axis=0)
        own_rows = w_own.shape[0]
        w_own = w_own * summed[:own_rows] / summed[own_rows][None, :]
    return (w_own, h_own)


def solution(mesh):
    in_specs = (
        P("samp", "kmer", None),
        P("samp", "kmer", None),
        P("samp", "kmer"),
        P("samp", "kmer", None, None, None),
        P(("samp", "kmer"), None),
        P(None, ("kmer", "samp")),
    )
    out_specs = (P(("samp", "kmer"), None), P(None, ("kmer", "samp")))
    return jax.shard_map(body, mesh=mesh, in_specs=in_specs, out_specs=out_specs, check_vma=False)
```

time: 581 us -> 205 us (0.35)
  blocking collectives: 538 us -> 126 us
  starting transfers between devices: 0.16 us -> 24.9 us
  waiting for transfers between devices: 0.07 us -> 19.3 us
  between operations: 14.6 us -> 1.67 us
    psum x4 -> x0, blocking collectives: 406 us -> none  [the longest x2 205 us: column_total(): lax.psum(jnp.sum(w_half.astype(jnp.float32), axis=0), ('samp', 'kmer'))]
    all_gather x5 -> x0, blocking collectives: 133 us -> none  [the longest x3 82.6 us: panel_of(): lax.all_gather(h_state.astype(jnp.bfloat16), 'samp', axis=1, tiled=True)]
    all_to_all x0 -> x7, blocking collectives: none -> 126 us  [the longest x3 49.3 us: spread(): lax.all_to_all(jnp.broadcast_to(x[None], (size,) + x.shape), axis_name, 0...]
    all_to_all x0 -> x2, starting transfers between devices: none -> 24.9 us  [spread(): lax.all_to_all(jnp.broadcast_to(x[None], (size,) + x.shape), axis_name, 0...]
    all_to_all x0 -> x2, waiting for transfers between devices: none -> 19.3 us  [spread(): lax.all_to_all(jnp.broadcast_to(x[None], (size,) + x.shape), axis_name, 0...]
  transfers between devices with their start and end apart: 4 -> 2, of which waited for: 0 -> 2; matrix products, arithmetic and copies ran while one was open for 0% -> 2% of each run, Pallas kernels for 0% -> 0%
where the time goes in v1:
time: 205 us; the launch traced here: 202 us
  blocking collectives  126 us (61%)
  starting transfers between devices  24.9 us (12%)
  waiting for transfers between devices  19.3 us (9%)
  matrix products  12.9 us (6%)
  local copies, waits for them, and re-layouts  9.78 us (5%)
  other arithmetic  7.3 us (4%)
    all_to_all x3, blocking collectives, spread(): lax.all_to_all(jnp.broadcast_to(x[None], (size,) + x.shape), axis_name, 0...  49.3 us
    all_to_all x2, blocking collectives, body(): lax.all_to_all(jnp.concatenate([numerator, col_rows], axis=1), 'samp', 0, 0)  47.2 us
    all_to_all x2, blocking collectives, body(): lax.all_to_all(jnp.concatenate([numerator, row_rows], axis=1), 'kmer', 0, 0)  29.8 us
    all_to_all x2, starting transfers between devices, spread(): lax.all_to_all(jnp.broadcast_to(x[None], (size,) + x.shape), axis_name, 0...  24.9 us
    all_to_all x2, waiting for transfers between devices, spread(): lax.all_to_all(jnp.broadcast_to(x[None], (size,) + x.shape), axis_name, 0...  19.3 us
    dot_general x2, matrix products, body(): jnp.einsum('gij,gkj->gik', ratio, h_tiles, preferred_element_type=jnp.flo...  5.03 us
  transfers between devices with their start and end apart: 2, of which 2 were waited for; matrix products, arithmetic and copies ran while one was open for 2% of the time, Pallas kernels for 0%

profile of v1, /device:TPU:1, one launch (start us, length us, event | category | flops | bytes accessed | tf_op | source)
XLA Modules:
  0.0 202.3 jit_solution(8996744766177975545)
XLA Ops:
  0.7 0.7 convert_element_type.57
  1.4 0.8 reshape.114
  2.2 15.7 %all-to-all-start = ((bf16[16,2,1024]{2,1,0:T(2,128)(2,1)}), bf16[16,2,1024]{2,1,0:T(2,128)(2,1)S(1)}, u32[]{:S(2)}, u32[]{:S(2)}) async-start(bf16[16,2,1024]{2,1,0:T(2,128)(2,1)} %reshape.114), calls=%async_computation | async-start | bytes 131072 | tf_op jit(solution)/shard_map/all_to_all | solution.py:14
  17.9 0.7 compare_select_fusion
  19.2 0.8 convert_element_type.58
  20.0 0.7 compare_select_fusion.1
  20.7 8.8 %all-to-all-done = bf16[16,2,1024]{2,1,0:T(2,128)(2,1)S(1)} async-done(((bf16[16,2,1024]{2,1,0:T(2,128)(2,1)}), bf16[16,2,1024]{2,1,0:T(2,128)(2,1)S(1)}, u32[]{:S(2)}, u32[]{:S(2)}) %all-to-all-start) | async-done | bytes 65568 | tf_op jit(solution)/shard_map/all_to_all | solution.py:14
  29.5 0.9 broadcast_in_dim.104
  30.4 9.2 %all-to-all-start.1 = ((bf16[32,64,128]{2,1,0:T(8,128)(2,1)}), bf16[32,64,128]{2,1,0:T(8,128)(2,1)S(1)}, u32[]{:S(2)}, u32[]{:S(2)}) async-start(bf16[32,64,128]{2,1,0:T(8,128)(2,1)} %broadcast_in_dim.104), calls=%async_computation.1 | async-start | bytes 1048576 | tf_op jit(solution)/shard_map/all_to_all | solution.py:14
  40.0 0.7 gather_fusion
  40.7 10.5 %all-to-all-done.1 = bf16[32,64,128]{2,1,0:T(8,128)(2,1)S(1)} async-done(((bf16[32,64,128]{2,1,0:T(8,128)(2,1)}), bf16[32,64,128]{2,1,0:T(8,128)(2,1)S(1)}, u32[]{:S(2)}, u32[]{:S(2)}) %all-to-all-start.1) | async-done | bytes 524320 | tf_op jit(solution)/shard_map/all_to_all | solution.py:14
  51.8 2.2 %fusion.9 = f32[32,64,128]{2,1,0:T(8,128)S(1)} fusion(bf16[1,1,32,128,128]{4,3,2,1,0:T(8,128)(2,1)} %param.13, pred[32]{0:T(512)(128)(4,1)S(1)} %iota_compare_fusion.2, bf16[32,64,128]{2,1,0:T(8,128)(2,1)S(1)} %gather_fusion.1, pred[32]{0:T(512)(128)(4,1)S(1)} %get-tuple-element.6, bf16[32,128,64]{1,2,0:T(8,128)(2,1)S(1)} %gather_fusion, ...), kind=kOutput, calls=%fused_computation.18 | convolution fusion | flops 137101312 | bytes 3145824 | tf_op jit(solution)/shard_map/gik,gij->gkj/dot_general | solution.py:46
  54.0 1.3 fusion.22
  55.4 0.7 copy.38
  56.1 22.5 %all_to_all.45 = f32[32,72,128]{2,1,0:T(8,128)S(1)} all-to-all(f32[32,72,128]{2,1,0:T(8,128)S(1)} %copy.38), channel_id=1, replica_groups=mesh['samp'=32,'kmer'=16] {'samp'}, dimensions={0} | all-to-all | bytes 2359296 | tf_op jit(solution)/shard_map/all_to_all | solution.py:54
  78.7 0.7 copy-done
  79.6 15.2 %all_to_all.46 = bf16[32,64,128]{2,1,0:T(8,128)(2,1)S(1)} all-to-all(bf16[32,64,128]{2,1,0:T(8,128)(2,1)S(1)} %broadcast_in_dim.107), channel_id=1, replica_groups=mesh['samp'=32,'kmer'=16] {'samp'}, dimensions={0} | all-to-all | bytes 1048576 | tf_op jit(solution)/shard_map/all_to_all | solution.py:14
  95.5 2.5 %fusion.11 = f32[32,128,64]{1,2,0:T(8,128)S(1)} fusion(bf16[1,1,32,128,128]{4,3,2,1,0:T(8,128)(2,1)} %param.13, pred[32]{0:T(512)(128)(4,1)S(1)} %iota_compare_fusion.2, bf16[32,128,64]{1,2,0:T(8,128)(2,1)S(1)} %gather_fusion, pred[32]{0:T(512)(128)(4,1)S(1)} %get-tuple-element.7, bf16[32,64,128]{2,1,0:T(8,128)(2,1)S(1)} %gather_fusion.2, ...), kind=kOutput, calls=%fused_computation.20 | convolution fusion | flops 137101312 | bytes 3145824 | tf_op jit(solution)/shard_map/gij,gkj->gik/dot_general | solution.py:62
  98.0 1.0 fusion.20
  99.6 14.9 %all_to_all.47 = f32[16,1,2560]{2,1,0:T(1,128)S(1)} all-to-all(f32[16,1,2560]{2,1,0:T(1,128)S(1)} %reshape.116), channel_id=1, replica_groups=mesh['samp'=32,'kmer'=16] {'kmer'}, dimensions={0} | all-to-all | bytes 327680 | tf_op jit(solution)/shard_map/all_to_all | solution.py:70
  115.0 1.0 reduce.2
  116.4 18.9 %all_to_all.48 = bf16[16,2,1024]{2,1,0:T(2,128)(2,1)S(1)} all-to-all(bf16[16,2,1024]{2,1,0:T(2,128)(2,1)S(1)} %reshape.118), channel_id=1, replica_groups=mesh['samp'=32,'kmer'=16] {'kmer'}, dimensions={0} | all-to-all | bytes 131072 | tf_op jit(solution)/shard_map/all_to_all | solution.py:14
  136.8 1.0 fusion.8
  137.8 1.3 fusion.18
  139.2 0.7 copy.43
  139.9 24.7 %all_to_all.49 = f32[32,72,128]{2,1,0:T(8,128)S(1)} all-to-all(f32[32,72,128]{2,1,0:T(8,128)S(1)} %copy.43), channel_id=1, replica_groups=mesh['samp'=32,'kmer'=16] {'samp'}, dimensions={0} | all-to-all | bytes 2359296 | tf_op jit(solution)/shard_map/all_to_all | solution.py:54
  164.7 0.7 fusion.72
  165.5 15.2 %all_to_all.50 = bf16[32,64,128]{2,1,0:T(8,128)(2,1)S(1)} all-to-all(bf16[32,64,128]{2,1,0:T(8,128)(2,1)S(1)} %broadcast_in_dim.111), channel_id=1, replica_groups=mesh['samp'=32,'kmer'=16] {'samp'}, dimensions={0} | all-to-all | bytes 1048576 | tf_op jit(solution)/shard_map/all_to_all | solution.py:14
  181.4 2.5 %fusion.10 = f32[32,128,64]{1,2,0:T(8,128)S(1)} fusion(bf16[1,1,32,128,128]{4,3,2,1,0:T(8,128)(2,1)} %param.13, pred[32]{0:T(512)(128)(4,1)S(1)} %iota_compare_fusion.2, bf16[32,64,128]{2,1,0:T(8,128)(2,1)S(1)} %gather_fusion.4, pred[32]{0:T(512)(128)(4,1)S(1)} %get-tuple-element.6, bf16[32,128,64]{1,2,0:T(8,128)(2,1)S(1)} %gather_fusion.3, ...), kind=kOutput, calls=%fused_computation.19 | convolution fusion | flops 137101312 | bytes 3145824 | tf_op jit(solution)/shard_map/gij,gkj->gik/dot_general | solution.py:62
  183.9 1.1 fusion.16
  185.5 14.9 %all_to_all.51 = f32[16,1,2560]{2,1,0:T(1,128)S(1)} all-to-all(f32[16,1,2560]{2,1,0:T(1,128)S(1)} %reshape.120), channel_id=1, replica_groups=mesh['samp'=32,'kmer'=16] {'kmer'}, dimensions={0} | all-to-all | bytes 327680 | tf_op jit(solution)/shard_map/all_to_all | solution.py:70
  200.4 1.0 reduce.3
  (58 shorter events, 7.1 us)
Async XLA Ops:
  0.6 39.0 %copy-start.2 = (s32[1,1,32]{2,1,0:T(1,128)S(1)}, s32[1,1,32]{2,1,0:T(1,128)}, u32[]{:S(2)}) copy-start(s32[1,1,32]{2,1,0:T(1,128)} %param.11) | copy-start | bytes 388
  0.6 39.0 %copy-start.3 = (s32[1,1,32]{2,1,0:T(1,128)S(1)}, s32[1,1,32]{2,1,0:T(1,128)}, u32[]{:S(2)}) copy-start(s32[1,1,32]{2,1,0:T(1,128)} %param.10) | copy-start | bytes 388
  2.2 27.3 %all-to-all-start = ((bf16[16,2,1024]{2,1,0:T(2,128)(2,1)}), bf16[16,2,1024]{2,1,0:T(2,128)(2,1)S(1)}, u32[]{:S(2)}, u32[]{:S(2)}) async-start(bf16[16,2,1024]{2,1,0:T(2,128)(2,1)} %reshape.114), calls=%async_computation | async-start | bytes 131072 | tf_op jit(solution)/shard_map/all_to_all | solution.py:14
  30.4 20.8 %all-to-all-start.1 = ((bf16[32,64,128]{2,1,0:T(8,128)(2,1)}), bf16[32,64,128]{2,1,0:T(8,128)(2,1)S(1)}, u32[]{:S(2)}, u32[]{:S(2)}) async-start(bf16[32,64,128]{2,1,0:T(8,128)(2,1)} %broadcast_in_dim.104), calls=%async_computation.1 | async-start | bytes 1048576 | tf_op jit(solution)/shard_map/all_to_all | solution.py:14
  78.6 0.8 copy-start
  99.4 16.9 %copy-start.1 = (f32[32,64]{1,0:T(8,128)S(1)}, f32[32,64]{1,0:T(8,128)}, u32[]{:S(2)}) copy-start(f32[32,64]{1,0:T(8,128)} %param.14) | copy-start | bytes 24580
  135.6 1.2 copy-start.4

commit v2 on v1

v2 whole, which is shorter than its diff:
```python
import functools

import jax
import jax.numpy as jnp
from jax import lax
from jax.experimental import pallas as pl
from jax.experimental.pallas import tpu as pltpu
from jax.sharding import PartitionSpec as P

TILE = 128
RANK = 64
ROW_TILES = 4
COL_TILES = 32
CAP = 32
ITERS = 2
N_KMER = 16
N_CHIP = 16
OWN = 16
SUMS = 8

CORES = [[2 * a, 2 * a + 1] for a in range(N_CHIP)]
CHIPS = [[2 * a + c for a in range(N_CHIP)] for c in range(2)]

f32 = jnp.float32
bf16 = jnp.bfloat16
VMEM = pl.BlockSpec(memory_space=pltpu.VMEM)
SMEM = pl.BlockSpec(memory_space=pltpu.SMEM)


def call(kernel, out_shape, in_specs, scratch=(), flops=0):
    return pl.pallas_call(
        kernel,
        out_shape=out_shape,
        in_specs=in_specs,
        out_specs=jax.tree.map(lambda _: VMEM, out_shape),
        scratch_shapes=scratch,
        compiler_params=pltpu.CompilerParams(vmem_limit_bytes=32 * 2**20),
    )


def same_rank(shape):
    rank = lax.broadcasted_iota(jnp.int32, shape, 0)
    lane = lax.broadcasted_iota(jnp.int32, shape, 1)
    return jnp.bitwise_and(lane, RANK - 1) == rank


def start_kernel(w_ref, h_ref, own_ref, w_out, h_out):
    own_ref[:, :RANK] = w_ref[:OWN, :]
    own_ref[:, RANK:] = w_ref[OWN:, :]
    half = own_ref[...].astype(bf16)
    for k in range(N_KMER):
        w_out[k] = half
    h_half = h_ref[...].astype(bf16)
    for k in range(N_CHIP):
        h_out[k] = h_half


def unpack(w_ref, tiles_ref):
    for k in range(N_KMER):
        r, q = k // 4, k % 4
        block = w_ref[k]
        tiles_ref[r, 32 * q : 32 * q + OWN, :] = block[:, :RANK]
        tiles_ref[r, 32 * q + OWN : 32 * q + 2 * OWN, :] = block[:, RANK:]


def ratio_of(g, rows, cols, count, values_ref, tiles_ref, h_ref):
    r, c = rows[g], cols[g]
    h_tile = h_ref[c & 1, c >> 1]
    estimate = jnp.dot(tiles_ref[r], h_tile, preferred_element_type=f32)
    ratio = values_ref[g].astype(f32) / estimate
    ratio = jnp.where(g < count[0], ratio, 0.0).astype(bf16)
    return r, c, h_tile, ratio


def numer_h_kernel(rows, cols, count, values_ref, w_ref, h_ref, out_ref, tiles_ref, flip_ref):
    unpack(w_ref, tiles_ref)
    for r in range(ROW_TILES):
        flip_ref[r] = tiles_ref[r].T
    sums = jnp.sum(w_ref[...].astype(f32).reshape(N_KMER * OWN, 2 * RANK), axis=0, keepdims=True)
    out_ref[:, :, :RANK, :] = jnp.zeros((2, N_CHIP, RANK, TILE), f32)
    out_ref[:, :, RANK:, :] = jnp.broadcast_to(sums[None, None], (2, N_CHIP, SUMS, TILE))
    for g in range(CAP):
        r, c, h_tile, ratio = ratio_of(g, rows, cols, count, values_ref, tiles_ref, h_ref)
        out_ref[c & 1, c >> 1, :RANK, :] += jnp.dot(flip_ref[r], ratio, preferred_element_type=f32)


def update_h_kernel(parts_ref, h_ref, own_ref, out_ref):
    summed = parts_ref[0]
    for k in range(1, N_CHIP):
        summed = summed + parts_ref[k]
    total = jnp.where(same_rank((RANK, TILE)), summed[RANK : RANK + 1], 0.0)
    h_new = h_ref[...] * summed[:RANK] / jnp.sum(total, axis=1, keepdims=True)
    own_ref[...] = h_new
    half = h_new.astype(bf16)
    for k in range(N_CHIP):
        out_ref[k] = half


def numer_w_kernel(rows, cols, count, values_ref, w_ref, h_ref, out_ref, tiles_ref, acc_ref):
    unpack(w_ref, tiles_ref)
    sums = jnp.zeros((RANK, TILE), f32)
    for c in range(COL_TILES):
        sums = sums + h_ref[c % 2, c // 2].astype(f32)
    sums = jnp.where(same_rank((RANK, TILE)), jnp.sum(sums, axis=1, keepdims=True), 0.0)
    sums = jnp.sum(sums, axis=0, keepdims=True)
    out_ref[:, OWN:, :] = jnp.broadcast_to(sums[None], (N_KMER, SUMS, TILE))
    acc_ref[...] = jnp.zeros_like(acc_ref)
    for g in range(CAP):
        r, c, h_tile, ratio = ratio_of(g, rows, cols, count, values_ref, tiles_ref, h_ref)
        acc_ref[r] += lax.dot_general(
            ratio, h_tile, (((1,), (1,)), ((), ())), preferred_element_type=f32
        )
    for k in range(N_KMER):
        r, q = k // 4, k % 4
        out_ref[k, :OWN, :RANK] = acc_ref[r, 32 * q : 32 * q + OWN, :]
        out_ref[k, :OWN, RANK:] = acc_ref[r, 32 * q + OWN : 32 * q + 2 * OWN, :]


def new_w(parts_ref, w_ref):
    summed = parts_ref[0]
    for k in range(1, N_KMER):
        summed = summed + parts_ref[k]
    return w_ref[...] * summed[:OWN] / summed[OWN : OWN + 1]


def update_w_kernel(parts_ref, w_ref, own_ref, out_ref):
    w_new = new_w(parts_ref, w_ref)
    own_ref[...] = w_new
    half = w_new.astype(bf16)
    for k in range(N_KMER):
        out_ref[k] = half


def last_w_kernel(parts_ref, w_ref, own_ref):
    w_new = new_w(parts_ref, w_ref)
    own_ref[:OWN, :] = w_new[:, :RANK]
    own_ref[OWN:, :] = w_new[:, RANK:]


def to_kmer(x):
    return lax.all_to_all(x, "kmer", 0, 0)


def to_chips(x):
    return lax.all_to_all(x, "samp", 0, 0, axis_index_groups=CHIPS)


def panel_of(spread):
    return lax.all_gather(to_chips(spread), "samp", axis=0, axis_index_groups=CORES)


def body(tile_rows, tile_cols, tile_count, tile_values, w_init, h_init):
    shape = jax.ShapeDtypeStruct
    slots = (tile_rows.reshape(-1), tile_cols.reshape(-1), tile_count.reshape(-1))
    values = tile_values.reshape(CAP, TILE, TILE)
    w_spread = shape((N_KMER, OWN, 2 * RANK), bf16)
    h_spread = shape((N_CHIP, RANK, TILE), bf16)
    w_own, h_own = shape((OWN, 2 * RANK), f32), shape((RANK, TILE), f32)
    tiles = pltpu.VMEM((ROW_TILES, TILE, RANK), bf16)
    flip = pltpu.VMEM((ROW_TILES, RANK, TILE), bf16)
    acc = pltpu.VMEM((ROW_TILES, TILE, RANK), f32)
    wide = [SMEM] * 3 + [VMEM] * 3

    start = call(start_kernel, (w_own, w_spread, h_spread), [VMEM] * 2)
    numer_h = call(numer_h_kernel, shape((2, N_CHIP, RANK + SUMS, TILE), f32), wide, [tiles, flip])
    update_h = call(update_h_kernel, (h_own, h_spread), [VMEM] * 2)
    numer_w = call(numer_w_kernel, shape((N_KMER, OWN + SUMS, TILE), f32), wide, [tiles, acc])
    update_w = call(update_w_kernel, (w_own, w_spread), [VMEM] * 2)
    last_w = call(last_w_kernel, shape((2 * OWN, RANK), f32), [VMEM] * 2)

    w_own, w_out, h_out = start(w_init, h_init)
    h_own = h_init
    w_panel = to_kmer(w_out)
    w_panel, h_out = lax.optimization_barrier((w_panel, h_out))
    h_panel = panel_of(h_out)
    for sweep in range(ITERS):
        numer = numer_h(*slots, values, w_panel, h_panel)
        halves = lax.all_to_all(numer, "samp", 0, 0, axis_index_groups=CORES)
        h_own, h_out = update_h(to_chips(halves[0] + halves[1]), h_own)
        h_panel = panel_of(h_out)
        parts = to_kmer(numer_w(*slots, values, w_panel, h_panel))
        if sweep < ITERS - 1:
            w_own, w_out = update_w(parts, w_own)
            w_panel = to_kmer(w_out)
    return last_w(parts, w_own), h_own


def solution(mesh):
    in_specs = (
        P("samp", "kmer", None),
        P("samp", "kmer", None),
        P("samp", "kmer"),
        P("samp", "kmer", None, None, None),
        P(("samp", "kmer"), None),
        P(None, ("kmer", "samp")),
    )
    out_specs = (P(("samp", "kmer"), None), P(None, ("kmer", "samp")))
    return jax.shard_map(body, mesh=mesh, in_specs=in_specs, out_specs=out_specs, check_vma=False)
```

time: 205 us -> 182 us (0.89)
  blocking collectives: 126 us -> 153 us
  starting transfers between devices: 24.9 us -> 6.76 us
  matrix products: 12.9 us -> 0 us
  waiting for transfers between devices: 19.3 us -> 6.89 us
  Pallas kernels: 0 us -> 8.45 us
  local copies, waits for them, and re-layouts: 9.78 us -> 1.57 us
  other arithmetic: 7.3 us -> 0.12 us
    all_to_all x2 -> x1, starting transfers between devices: 24.9 us -> 6.76 us  [to_chips(): return lax.all_to_all(x, 'samp', 0, 0, axis_index_groups=CHIPS)]
    all_gather x0 -> x3, blocking collectives: none -> 14.4 us  [panel_of(): lax.all_gather(to_chips(spread), 'samp', axis=0, axis_index_groups=CORES)]
    dot_general x8 -> x0, matrix products: 12.9 us -> none  [the longest x2 5.03 us: body(): jnp.einsum('gij,gkj->gik', ratio, h_tiles, preferred_element_type=jnp.flo...]
    all_to_all x7 -> x10, blocking collectives: 126 us -> 139 us  [the longest x4 77.9 us: to_kmer(): return lax.all_to_all(x, 'kmer', 0, 0)]
    all_to_all x2 -> x1, waiting for transfers between devices: 19.3 us -> 6.89 us  [to_chips(): return lax.all_to_all(x, 'samp', 0, 0, axis_index_groups=CHIPS)]
    pallas_call x0 -> x9, Pallas kernels: none -> 8.45 us  [the longest x2 3.11 us: body(): parts = to_kmer(numer_w(*slots, values, w_panel, h_panel))]
    gather x5 -> x0, local copies, waits for them, and re-layouts: 3.24 us -> none  [the longest x3 1.94 us: body(): h_tiles = jnp.take(h_panel, col_index, axis=0)]
    convert_element_type x5 -> x0, other arithmetic: 2.29 us -> none  [the longest x3 1.56 us: body(): h_panel = spread(h_own.astype(jnp.bfloat16), 'samp', N_SAMP)]
  transfers between devices with their start and end apart: 2 -> 1, of which waited for: 2 -> 1; matrix products, arithmetic and copies ran while one was open for 2% -> 0% of each run, Pallas kernels for 0% -> 0%
where the time goes in v2:
time: 182 us; the launch traced here: 178 us
  blocking collectives  153 us (84%)
  Pallas kernels  8.45 us (5%)
  waiting for transfers between devices  6.89 us (4%)
  starting transfers between devices  6.76 us (4%)
    all_to_all x4, blocking collectives, to_kmer(): return lax.all_to_all(x, 'kmer', 0, 0)  77.9 us
    all_to_all x4, blocking collectives, to_chips(): return lax.all_to_all(x, 'samp', 0, 0, axis_index_groups=CHIPS)  49.9 us
    all_gather x3, blocking collectives, panel_of(): lax.all_gather(to_chips(spread), 'samp', axis=0, axis_index_groups=CORES)  14.4 us
    all_to_all x2, blocking collectives, body(): halves = lax.all_to_all(numer, 'samp', 0, 0, axis_index_groups=CORES)  11.2 us
    all_to_all x1, waiting for transfers between devices, to_chips(): return lax.all_to_all(x, 'samp', 0, 0, axis_index_groups=CHIPS)  6.89 us
    all_to_all x1, starting transfers between devices, to_chips(): return lax.all_to_all(x, 'samp', 0, 0, axis_index_groups=CHIPS)  6.76 us
  transfers between devices with their start and end apart: 1, of which 1 were waited for; matrix products, arithmetic and copies ran while one was open for 0% of the time, Pallas kernels for 0%

profile of v2, /device:TPU:1, one launch (start us, length us, event | category | flops | bytes accessed | tf_op | source)
XLA Modules:
  0.0 178.4 jit_solution(17500283299433868656)
XLA Ops:
  0.6 0.0 copy-start
  0.6 0.0 copy-start.1
  0.7 0.8 copy-done.1
  1.5 0.7 copy-done.3
  2.2 0.7 shard_map.77
  2.9 27.1 %all_to_all.55.w_ref = bf16[16,16,128]{2,1,0:T(8,128)(2,1)S(1)} all-to-all(bf16[16,16,128]{2,1,0:T(8,128)(2,1)S(1)} %get-tuple-element.13), channel_id=1, replica_groups=mesh['samp'=32,'kmer'=16] {'kmer'}, dimensions={0} | all-to-all | bytes 131072 | tf_op jit(solution)/shard_map/all_to_all | solution.py:141
  30.0 6.8 %all-to-all-start.1 = ((bf16[16,64,128]{2,1,0:T(8,128)(2,1)}), bf16[16,64,128]{2,1,0:T(8,128)(2,1)S(1)}, u32[]{:S(2)}, u32[]{:S(2)}) async-start(bf16[16,64,128]{2,1,0:T(8,128)(2,1)} %get-tuple-element.16), calls=%async_computation.1 | async-start | bytes 524288 | tf_op jit(solution)/shard_map/all_to_all | solution.py:145
  37.5 6.9 %all-to-all-done.1 = bf16[16,64,128]{2,1,0:T(8,128)(2,1)S(1)} async-done(((bf16[16,64,128]{2,1,0:T(8,128)(2,1)}), bf16[16,64,128]{2,1,0:T(8,128)(2,1)S(1)}, u32[]{:S(2)}, u32[]{:S(2)}) %all-to-all-start.1) | async-done | bytes 262176 | tf_op jit(solution)/shard_map/all_to_all | solution.py:145
  44.3 5.3 %all-gather = bf16[32,64,128]{2,1,0:T(8,128)(2,1)S(1)} all-gather(bf16[16,64,128]{2,1,0:T(8,128)(2,1)S(1)} %all-to-all-done.1), channel_id=2, replica_groups={{0,16},{32,48},{64,80},{96,112},{128,144},{160,176},{192,208},{224,240}..., dimensions={0}, use_global_device_ids=true | all-gather | bytes 786432 | tf_op jit(solution)/shard_map/all_gather | solution.py:149
  49.7 0.0 copy-done
  49.7 0.0 copy-done.4
  49.7 0.0 copy-done.5
  49.7 1.5 shard_map.78
  51.2 4.7 %all_to_all.56 = f32[2,16,72,128]{3,2,1,0:T(8,128)S(1)} all-to-all(f32[2,16,72,128]{3,2,1,0:T(8,128)S(1)} %shard_map.78), channel_id=1, replica_groups={{0,16},{32,48},{64,80},{96,112},{128,144},{160,176},{192,208},{224,240}..., dimensions={0} | all-to-all | bytes 2359296 | tf_op jit(solution)/shard_map/all_to_all | solution.py:178
  55.9 0.1 fusion.1
  56.0 14.0 %all_to_all.57.parts_ref = f32[16,72,128]{2,1,0:T(8,128)S(1)} all-to-all(f32[16,72,128]{2,1,0:T(8,128)S(1)} %fusion.1), channel_id=1, replica_groups={{0,32,64,96,128,160,192,224,256,288,320,352,384,416,448,480},{16,48,80,..., dimensions={0} | all-to-all | bytes 1179648 | tf_op jit(solution)/shard_map/all_to_all | solution.py:145
  70.0 0.1 shard_map.79
  70.1 10.9 %all_to_all.58 = bf16[16,64,128]{2,1,0:T(8,128)(2,1)S(1)} all-to-all(bf16[16,64,128]{2,1,0:T(8,128)(2,1)S(1)} %get-tuple-element.17), channel_id=1, replica_groups={{0,32,64,96,128,160,192,224,256,288,320,352,384,416,448,480},{16,48,80,..., dimensions={0} | all-to-all | bytes 524288 | tf_op jit(solution)/shard_map/all_to_all | solution.py:145
  81.0 4.5 %all-gather.1 = bf16[32,64,128]{2,1,0:T(8,128)(2,1)S(1)} all-gather(bf16[16,64,128]{2,1,0:T(8,128)(2,1)S(1)} %all_to_all.58), channel_id=3, replica_groups={{0,16},{32,48},{64,80},{96,112},{128,144},{160,176},{192,208},{224,240}..., dimensions={0}, use_global_device_ids=true | all-gather | bytes 786432 | tf_op jit(solution)/shard_map/all_gather | solution.py:149
  85.6 1.5 shard_map.80
  87.1 15.5 %all_to_all.59.parts_ref = f32[16,24,128]{2,1,0:T(8,128)S(1)} all-to-all(f32[16,24,128]{2,1,0:T(8,128)S(1)} %shard_map.80), channel_id=1, replica_groups=mesh['samp'=32,'kmer'=16] {'kmer'}, dimensions={0} | all-to-all | bytes 393216 | tf_op jit(solution)/shard_map/all_to_all | solution.py:141
  102.7 19.7 %all_to_all.60.w_ref = bf16[16,16,128]{2,1,0:T(8,128)(2,1)S(1)} all-to-all(bf16[16,16,128]{2,1,0:T(8,128)(2,1)S(1)} %get-tuple-element.19), channel_id=1, replica_groups=mesh['samp'=32,'kmer'=16] {'kmer'}, dimensions={0} | all-to-all | bytes 131072 | tf_op jit(solution)/shard_map/all_to_all | solution.py:141
  122.3 1.5 shard_map.82
  123.9 6.5 %all_to_all.61 = f32[2,16,72,128]{3,2,1,0:T(8,128)S(1)} all-to-all(f32[2,16,72,128]{3,2,1,0:T(8,128)S(1)} %shard_map.82), channel_id=1, replica_groups={{0,16},{32,48},{64,80},{96,112},{128,144},{160,176},{192,208},{224,240}..., dimensions={0} | all-to-all | bytes 2359296 | tf_op jit(solution)/shard_map/all_to_all | solution.py:178
  130.3 0.1 fusion
  130.4 14.0 %all_to_all.62.parts_ref = f32[16,72,128]{2,1,0:T(8,128)S(1)} all-to-all(f32[16,72,128]{2,1,0:T(8,128)S(1)} %fusion), channel_id=1, replica_groups={{0,32,64,96,128,160,192,224,256,288,320,352,384,416,448,480},{16,48,80,..., dimensions={0} | all-to-all | bytes 1179648 | tf_op jit(solution)/shard_map/all_to_all | solution.py:145
  144.4 0.7 shard_map.83
  145.2 10.9 %all_to_all.63 = bf16[16,64,128]{2,1,0:T(8,128)(2,1)S(1)} all-to-all(bf16[16,64,128]{2,1,0:T(8,128)(2,1)S(1)} %get-tuple-element.21), channel_id=1, replica_groups={{0,32,64,96,128,160,192,224,256,288,320,352,384,416,448,480},{16,48,80,..., dimensions={0} | all-to-all | bytes 524288 | tf_op jit(solution)/shard_map/all_to_all | solution.py:145
  156.1 4.5 %all-gather.2 = bf16[32,64,128]{2,1,0:T(8,128)(2,1)S(1)} all-gather(bf16[16,64,128]{2,1,0:T(8,128)(2,1)S(1)} %all_to_all.63), channel_id=4, replica_groups={{0,16},{32,48},{64,80},{96,112},{128,144},{160,176},{192,208},{224,240}..., dimensions={0}, use_global_device_ids=true | all-gather | bytes 786432 | tf_op jit(solution)/shard_map/all_gather | solution.py:149
  160.6 1.6 shard_map.84
  162.2 15.6 %all_to_all.64.parts_ref = f32[16,24,128]{2,1,0:T(8,128)S(1)} all-to-all(f32[16,24,128]{2,1,0:T(8,128)S(1)} %shard_map.84), channel_id=1, replica_groups=mesh['samp'=32,'kmer'=16] {'kmer'}, dimensions={0} | all-to-all | bytes 393216 | tf_op jit(solution)/shard_map/all_to_all | solution.py:141
  177.7 0.7 shard_map.85
  (6 shorter events, 0.0 us)
Async XLA Ops:
  0.6 49.1 %copy-start = (bf16[1,1,32,128,128]{4,3,2,1,0:T(8,128)(2,1)S(1)}, bf16[1,1,32,128,128]{4,3,2,1,0:T(8,128)(2,1)}, u32[]{:S(2)}) copy-start(bf16[1,1,32,128,128]{4,3,2,1,0:T(8,128)(2,1)} %param.9) | copy-start | bytes 3145732
  0.6 0.8 copy-start.1
  1.5 0.7 copy-start.3
  2.2 47.5 %copy-start.4 = (s32[1,1,32]{2,1,0:T(1,128)S(1)}, s32[1,1,32]{2,1,0:T(1,128)}, u32[]{:S(2)}) copy-start(s32[1,1,32]{2,1,0:T(1,128)} %param.6) | copy-start | bytes 388
  2.2 47.5 %copy-start.5 = (s32[1,1,32]{2,1,0:T(1,128)S(1)}, s32[1,1,32]{2,1,0:T(1,128)}, u32[]{:S(2)}) copy-start(s32[1,1,32]{2,1,0:T(1,128)} %param.7) | copy-start | bytes 388
  30.0 14.3 %all-to-all-start.1 = ((bf16[16,64,128]{2,1,0:T(8,128)(2,1)}), bf16[16,64,128]{2,1,0:T(8,128)(2,1)S(1)}, u32[]{:S(2)}, u32[]{:S(2)}) async-start(bf16[16,64,128]{2,1,0:T(8,128)(2,1)} %get-tuple-element.16), calls=%async_computation.1 | async-start | bytes 524288 | tf_op jit(solution)/shard_map/all_to_all | solution.py:145
  55.9 14.1 %copy-start.2 = (f32[64,128]{1,0:T(8,128)S(1)}, f32[64,128]{1,0:T(8,128)}, u32[]{:S(2)}) copy-start(f32[64,128]{1,0:T(8,128)} %h_ref.3) | copy-start | bytes 98308

commit v3 on v2

--- a/solution.py
+++ b/solution.py
@@ -17,6 +17,8 @@
 N_CHIP = 16
 OWN = 16
 SUMS = 8
+QUAD = 4
+QUADS = OWN // QUAD + 1
 
 CORES = [[2 * a, 2 * a + 1] for a in range(N_CHIP)]
 CHIPS = [[2 * a + c for a in range(N_CHIP)] for c in range(2)]
@@ -25,9 +27,10 @@
 bf16 = jnp.bfloat16
 VMEM = pl.BlockSpec(memory_space=pltpu.VMEM)
 SMEM = pl.BlockSpec(memory_space=pltpu.SMEM)
-
-
-def call(kernel, out_shape, in_specs, scratch=(), flops=0):
+HBM = pl.BlockSpec(memory_space=pltpu.HBM)
+
+
+def call(kernel, out_shape, in_specs, scratch=()):
     return pl.pallas_call(
         kernel,
         out_shape=out_shape,
@@ -44,12 +47,20 @@
     return jnp.bitwise_and(lane, RANK - 1) == rank
 
 
-def start_kernel(w_ref, h_ref, own_ref, w_out, h_out):
+def start_kernel(count, w_any, h_any, own_ref, w_out, h_out, live_ref, w_ref, h_ref, sems):
+    w_copy = pltpu.make_async_copy(w_any, w_ref, sems.at[0])
+    h_copy = pltpu.make_async_copy(h_any, h_ref, sems.at[1])
+    w_copy.start()
+    h_copy.start()
+    slot = lax.broadcasted_iota(jnp.int32, (CAP, TILE), 0)
+    live_ref[...] = (slot < count[0, 0]).astype(f32)
+    w_copy.wait()
     own_ref[:, :RANK] = w_ref[:OWN, :]
     own_ref[:, RANK:] = w_ref[OWN:, :]
     half = own_ref[...].astype(bf16)
     for k in range(N_KMER):
         w_out[k] = half
+    h_copy.wait()
     h_half = h_ref[...].astype(bf16)
     for k in range(N_CHIP):
         h_out[k] = h_half
@@ -63,16 +74,16 @@
         tiles_ref[r, 32 * q + OWN : 32 * q + 2 * OWN, :] = block[:, RANK:]
 
 
-def ratio_of(g, rows, cols, count, values_ref, tiles_ref, h_ref):
-    r, c = rows[g], cols[g]
+def ratio_of(g, rows, cols, live_ref, values_ref, tiles_ref, h_ref):
+    r, c = rows[0, 0, g], cols[0, 0, g]
     h_tile = h_ref[c & 1, c >> 1]
     estimate = jnp.dot(tiles_ref[r], h_tile, preferred_element_type=f32)
     ratio = values_ref[g].astype(f32) / estimate
-    ratio = jnp.where(g < count[0], ratio, 0.0).astype(bf16)
+    ratio = jnp.where(live_ref[g : g + 1, :] > 0.0, ratio, 0.0).astype(bf16)
     return r, c, h_tile, ratio
 
 
-def numer_h_kernel(rows, cols, count, values_ref, w_ref, h_ref, out_ref, tiles_ref, flip_ref):
+def numer_h_kernel(rows, cols, live_ref, values_ref, w_ref, h_ref, out_ref, tiles_ref, flip_ref):
     unpack(w_ref, tiles_ref)
     for r in range(ROW_TILES):
         flip_ref[r] = tiles_ref[r].T
@@ -80,7 +91,7 @@
     out_ref[:, :, :RANK, :] = jnp.zeros((2, N_CHIP, RANK, TILE), f32)
     out_ref[:, :, RANK:, :] = jnp.broadcast_to(sums[None, None], (2, N_CHIP, SUMS, TILE))
     for g in range(CAP):
-        r, c, h_tile, ratio = ratio_of(g, rows, cols, count, values_ref, tiles_ref, h_ref)
+        r, c, h_tile, ratio = ratio_of(g, rows, cols, live_ref, values_ref, tiles_ref, h_ref)
         out_ref[c & 1, c >> 1, :RANK, :] += jnp.dot(flip_ref[r], ratio, preferred_element_type=f32)
 
 
@@ -96,43 +107,47 @@
         out_ref[k] = half
 
 
-def numer_w_kernel(rows, cols, count, values_ref, w_ref, h_ref, out_ref, tiles_ref, acc_ref):
+def numer_w_kernel(rows, cols, live_ref, values_ref, w_ref, h_ref, out_ref, tiles_ref, acc_ref):
     unpack(w_ref, tiles_ref)
     sums = jnp.zeros((RANK, TILE), f32)
     for c in range(COL_TILES):
         sums = sums + h_ref[c % 2, c // 2].astype(f32)
     sums = jnp.where(same_rank((RANK, TILE)), jnp.sum(sums, axis=1, keepdims=True), 0.0)
     sums = jnp.sum(sums, axis=0, keepdims=True)
-    out_ref[:, OWN:, :] = jnp.broadcast_to(sums[None], (N_KMER, SUMS, TILE))
+    out_ref[:, QUADS - 1] = jnp.broadcast_to(sums[None], (N_KMER, QUAD, TILE))
     acc_ref[...] = jnp.zeros_like(acc_ref)
     for g in range(CAP):
-        r, c, h_tile, ratio = ratio_of(g, rows, cols, count, values_ref, tiles_ref, h_ref)
+        r, c, h_tile, ratio = ratio_of(g, rows, cols, live_ref, values_ref, tiles_ref, h_ref)
         acc_ref[r] += lax.dot_general(
             ratio, h_tile, (((1,), (1,)), ((), ())), preferred_element_type=f32
         )
     for k in range(N_KMER):
         r, q = k // 4, k % 4
-        out_ref[k, :OWN, :RANK] = acc_ref[r, 32 * q : 32 * q + OWN, :]
-        out_ref[k, :OWN, RANK:] = acc_ref[r, 32 * q + OWN : 32 * q + 2 * OWN, :]
-
-
-def new_w(parts_ref, w_ref):
+        for a in range(OWN // QUAD):
+            row = 32 * q + QUAD * a
+            out_ref[k, a, :, :RANK] = acc_ref[r, row : row + QUAD, :]
+            out_ref[k, a, :, RANK:] = acc_ref[r, row + OWN : row + OWN + QUAD, :]
+
+
+def new_w(parts_ref, w_ref, rows_ref):
     summed = parts_ref[0]
     for k in range(1, N_KMER):
         summed = summed + parts_ref[k]
-    return w_ref[...] * summed[:OWN] / summed[OWN : OWN + 1]
-
-
-def update_w_kernel(parts_ref, w_ref, own_ref, out_ref):
-    w_new = new_w(parts_ref, w_ref)
+    for a in range(OWN // QUAD):
+        rows_ref[QUAD * a : QUAD * a + QUAD, :] = summed[a]
+    return w_ref[...] * rows_ref[...] / summed[QUADS - 1, :1]
+
+
+def update_w_kernel(parts_ref, w_ref, own_ref, out_ref, rows_ref):
+    w_new = new_w(parts_ref, w_ref, rows_ref)
     own_ref[...] = w_new
     half = w_new.astype(bf16)
     for k in range(N_KMER):
         out_ref[k] = half
 
 
-def last_w_kernel(parts_ref, w_ref, own_ref):
-    w_new = new_w(parts_ref, w_ref)
+def last_w_kernel(parts_ref, w_ref, own_ref, rows_ref):
+    w_new = new_w(parts_ref, w_ref, rows_ref)
     own_ref[:OWN, :] = w_new[:, :RANK]
     own_ref[OWN:, :] = w_new[:, RANK:]
 
@@ -151,7 +166,6 @@
 
 def body(tile_rows, tile_cols, tile_count, tile_values, w_init, h_init):
     shape = jax.ShapeDtypeStruct
-    slots = (tile_rows.reshape(-1), tile_cols.reshape(-1), tile_count.reshape(-1))
     values = tile_values.reshape(CAP, TILE, TILE)
     w_spread = shape((N_KMER, OWN, 2 * RANK), bf16)
     h_spread = shape((N_CHIP, RANK, TILE), bf16)
@@ -159,16 +173,20 @@
     tiles = pltpu.VMEM((ROW_TILES, TILE, RANK), bf16)
     flip = pltpu.VMEM((ROW_TILES, RANK, TILE), bf16)
     acc = pltpu.VMEM((ROW_TILES, TILE, RANK), f32)
-    wide = [SMEM] * 3 + [VMEM] * 3
-
-    start = call(start_kernel, (w_own, w_spread, h_spread), [VMEM] * 2)
+    rows = pltpu.VMEM((OWN, 2 * RANK), f32)
+    fetched = [pltpu.VMEM(w_init.shape, f32), pltpu.VMEM(h_init.shape, f32), pltpu.SemaphoreType.DMA((2,))]
+    wide = [SMEM] * 2 + [VMEM] * 4
+
+    live = shape((CAP, TILE), f32)
+    start = call(start_kernel, (w_own, w_spread, h_spread, live), [SMEM] + [HBM] * 2, fetched)
     numer_h = call(numer_h_kernel, shape((2, N_CHIP, RANK + SUMS, TILE), f32), wide, [tiles, flip])
     update_h = call(update_h_kernel, (h_own, h_spread), [VMEM] * 2)
-    numer_w = call(numer_w_kernel, shape((N_KMER, OWN + SUMS, TILE), f32), wide, [tiles, acc])
-    update_w = call(update_w_kernel, (w_own, w_spread), [VMEM] * 2)
-    last_w = call(last_w_kernel, shape((2 * OWN, RANK), f32), [VMEM] * 2)
-
-    w_own, w_out, h_out = start(w_init, h_init)
+    numer_w = call(numer_w_kernel, shape((N_KMER, QUADS, QUAD, TILE), f32), wide, [tiles, acc])
+    update_w = call(update_w_kernel, (w_own, w_spread), [VMEM] * 2, [rows])
+    last_w = call(last_w_kernel, shape((2 * OWN, RANK), f32), [VMEM] * 2, [rows])
+
+    w_own, w_out, h_out, live = start(tile_count, w_init, h_init)
+    slots = (tile_rows, tile_cols, live)
     h_own = h_init
     w_panel = to_kmer(w_out)
     w_panel, h_out = lax.optimization_barrier((w_panel, h_out))

time: 182 us -> 179 us (0.984)
  blocking collectives: 153 us -> 165 us
  waiting for transfers between devices: 6.89 us -> 0 us
  starting transfers between devices: 6.76 us -> 0 us
    all_to_all x4 -> x5, blocking collectives: 49.9 us -> 64 us  [to_chips(): return lax.all_to_all(x, 'samp', 0, 0, axis_index_groups=CHIPS)]
    all_to_all x1 -> x0, waiting for transfers between devices: 6.89 us -> none  [to_chips(): return lax.all_to_all(x, 'samp', 0, 0, axis_index_groups=CHIPS)]
    all_to_all x1 -> x0, starting transfers between devices: 6.76 us -> none  [to_chips(): return lax.all_to_all(x, 'samp', 0, 0, axis_index_groups=CHIPS)]
    all_to_all x4, blocking collectives: 77.9 us -> 75.8 us  [to_kmer(): return lax.all_to_all(x, 'kmer', 0, 0)]
  transfers between devices with their start and end apart: 1 -> 0, of which waited for: 1 -> 0; matrix products, arithmetic and copies ran while one was open for 0% -> 0% of each run, Pallas kernels for 0% -> 0%
where the time goes in v3:
time: 179 us; the launch traced here: 176 us
  blocking collectives  165 us (92%)
  Pallas kernels  8.01 us (4%)
    all_to_all x4, blocking collectives, to_kmer(): return lax.all_to_all(x, 'kmer', 0, 0)  75.8 us
    all_to_all x5, blocking collectives, to_chips(): return lax.all_to_all(x, 'samp', 0, 0, axis_index_groups=CHIPS)  64 us
    all_gather x3, blocking collectives, panel_of(): lax.all_gather(to_chips(spread), 'samp', axis=0, axis_index_groups=CORES)  14.4 us
    all_to_all x2, blocking collectives, body(): halves = lax.all_to_all(numer, 'samp', 0, 0, axis_index_groups=CORES)  11.2 us

profile of v3, /device:TPU:1, one launch (start us, length us, event | category | flops | bytes accessed | tf_op | source)
XLA Modules:
  0.0 176.3 jit_solution(16663071546918286098)
XLA Ops:
  0.6 0.0 copy-start
  1.4 0.0 copy-start.1
  1.4 0.7 copy-done.1
  2.1 0.7 copy-done.3
  2.9 0.2 shard_map.77
  3.0 27.1 %all_to_all.55.w_ref = bf16[16,16,128]{2,1,0:T(8,128)(2,1)S(1)} all-to-all(bf16[16,16,128]{2,1,0:T(8,128)(2,1)S(1)} %get-tuple-element.15), channel_id=1, replica_groups=mesh['samp'=32,'kmer'=16] {'kmer'}, dimensions={0} | all-to-all | bytes 131072 | tf_op jit(solution)/shard_map/all_to_all | solution.py:156
  30.2 14.1 %all_to_all.56 = bf16[16,64,128]{2,1,0:T(8,128)(2,1)S(1)} all-to-all(bf16[16,64,128]{2,1,0:T(8,128)(2,1)S(1)} %get-tuple-element.18), channel_id=1, replica_groups={{0,32,64,96,128,160,192,224,256,288,320,352,384,416,448,480},{16,48,80,..., dimensions={0} | all-to-all | bytes 524288 | tf_op jit(solution)/shard_map/all_to_all | solution.py:160
  44.2 5.3 %all-gather = bf16[32,64,128]{2,1,0:T(8,128)(2,1)S(1)} all-gather(bf16[16,64,128]{2,1,0:T(8,128)(2,1)S(1)} %all_to_all.56), channel_id=2, replica_groups={{0,16},{32,48},{64,80},{96,112},{128,144},{160,176},{192,208},{224,240}..., dimensions={0}, use_global_device_ids=true | all-gather | bytes 786432 | tf_op jit(solution)/shard_map/all_gather | solution.py:164
  49.6 0.0 copy-done
  49.6 0.0 copy-done.4
  49.6 0.0 copy-done.5
  49.6 1.5 shard_map.78
  51.1 4.7 %all_to_all.57 = f32[2,16,72,128]{3,2,1,0:T(8,128)S(1)} all-to-all(f32[2,16,72,128]{3,2,1,0:T(8,128)S(1)} %shard_map.78), channel_id=1, replica_groups={{0,16},{32,48},{64,80},{96,112},{128,144},{160,176},{192,208},{224,240}..., dimensions={0} | all-to-all | bytes 2359296 | tf_op jit(solution)/shard_map/all_to_all | solution.py:196
  55.8 0.1 fusion.1
  55.9 14.0 %all_to_all.58.parts_ref = f32[16,72,128]{2,1,0:T(8,128)S(1)} all-to-all(f32[16,72,128]{2,1,0:T(8,128)S(1)} %fusion.1), channel_id=1, replica_groups={{0,32,64,96,128,160,192,224,256,288,320,352,384,416,448,480},{16,48,80,..., dimensions={0} | all-to-all | bytes 1179648 | tf_op jit(solution)/shard_map/all_to_all | solution.py:160
  69.9 0.0 copy-done.2
  69.9 0.1 shard_map.79
  70.0 10.9 %all_to_all.59 = bf16[16,64,128]{2,1,0:T(8,128)(2,1)S(1)} all-to-all(bf16[16,64,128]{2,1,0:T(8,128)(2,1)S(1)} %get-tuple-element.19), channel_id=1, replica_groups={{0,32,64,96,128,160,192,224,256,288,320,352,384,416,448,480},{16,48,80,..., dimensions={0} | all-to-all | bytes 524288 | tf_op jit(solution)/shard_map/all_to_all | solution.py:160
  80.9 4.5 %all-gather.1 = bf16[32,64,128]{2,1,0:T(8,128)(2,1)S(1)} all-gather(bf16[16,64,128]{2,1,0:T(8,128)(2,1)S(1)} %all_to_all.59), channel_id=3, replica_groups={{0,16},{32,48},{64,80},{96,112},{128,144},{160,176},{192,208},{224,240}..., dimensions={0}, use_global_device_ids=true | all-gather | bytes 786432 | tf_op jit(solution)/shard_map/all_gather | solution.py:164
  85.5 1.6 shard_map.80
  87.0 14.9 %all_to_all.60.parts_ref = f32[16,5,4,128]{3,2,1,0:T(4,128)S(1)} all-to-all(f32[16,5,4,128]{3,2,1,0:T(4,128)S(1)} %shard_map.80), channel_id=1, replica_groups=mesh['samp'=32,'kmer'=16] {'kmer'}, dimensions={0} | all-to-all | bytes 327680 | tf_op jit(solution)/shard_map/all_to_all | solution.py:156
  102.0 18.9 %all_to_all.61.w_ref = bf16[16,16,128]{2,1,0:T(8,128)(2,1)S(1)} all-to-all(bf16[16,16,128]{2,1,0:T(8,128)(2,1)S(1)} %get-tuple-element.21), channel_id=1, replica_groups=mesh['samp'=32,'kmer'=16] {'kmer'}, dimensions={0} | all-to-all | bytes 131072 | tf_op jit(solution)/shard_map/all_to_all | solution.py:156
  120.8 1.5 shard_map.82
  122.4 6.5 %all_to_all.62 = f32[2,16,72,128]{3,2,1,0:T(8,128)S(1)} all-to-all(f32[2,16,72,128]{3,2,1,0:T(8,128)S(1)} %shard_map.82), channel_id=1, replica_groups={{0,16},{32,48},{64,80},{96,112},{128,144},{160,176},{192,208},{224,240}..., dimensions={0} | all-to-all | bytes 2359296 | tf_op jit(solution)/shard_map/all_to_all | solution.py:196
  128.9 0.1 fusion
  129.0 14.0 %all_to_all.63.parts_ref = f32[16,72,128]{2,1,0:T(8,128)S(1)} all-to-all(f32[16,72,128]{2,1,0:T(8,128)S(1)} %fusion), channel_id=1, replica_groups={{0,32,64,96,128,160,192,224,256,288,320,352,384,416,448,480},{16,48,80,..., dimensions={0} | all-to-all | bytes 1179648 | tf_op jit(solution)/shard_map/all_to_all | solution.py:160
  143.0 0.7 shard_map.83
  143.7 10.9 %all_to_all.64 = bf16[16,64,128]{2,1,0:T(8,128)(2,1)S(1)} all-to-all(bf16[16,64,128]{2,1,0:T(8,128)(2,1)S(1)} %get-tuple-element.23), channel_id=1, replica_groups={{0,32,64,96,128,160,192,224,256,288,320,352,384,416,448,480},{16,48,80,..., dimensions={0} | all-to-all | bytes 524288 | tf_op jit(solution)/shard_map/all_to_all | solution.py:160
  154.6 4.5 %all-gather.2 = bf16[32,64,128]{2,1,0:T(8,128)(2,1)S(1)} all-gather(bf16[16,64,128]{2,1,0:T(8,128)(2,1)S(1)} %all_to_all.64), channel_id=4, replica_groups={{0,16},{32,48},{64,80},{96,112},{128,144},{160,176},{192,208},{224,240}..., dimensions={0}, use_global_device_ids=true | all-gather | bytes 786432 | tf_op jit(solution)/shard_map/all_gather | solution.py:164
  159.1 1.6 shard_map.84
  160.7 14.9 %all_to_all.65.parts_ref = f32[16,5,4,128]{3,2,1,0:T(4,128)S(1)} all-to-all(f32[16,5,4,128]{3,2,1,0:T(4,128)S(1)} %shard_map.84), channel_id=1, replica_groups=mesh['samp'=32,'kmer'=16] {'kmer'}, dimensions={0} | all-to-all | bytes 327680 | tf_op jit(solution)/shard_map/all_to_all | solution.py:156
  175.6 0.7 shard_map.85
  (5 shorter events, 0.0 us)
Async XLA Ops:
  0.6 49.0 %copy-start = (bf16[1,1,32,128,128]{4,3,2,1,0:T(8,128)(2,1)S(1)}, bf16[1,1,32,128,128]{4,3,2,1,0:T(8,128)(2,1)}, u32[]{:S(2)}) copy-start(bf16[1,1,32,128,128]{4,3,2,1,0:T(8,128)(2,1)} %param.9) | copy-start | bytes 3145732
  1.4 0.8 copy-start.1
  2.1 0.7 copy-start.3
  2.9 46.7 %copy-start.4 = (s32[1,1,32]{2,1,0:T(1,128)S(1)}, s32[1,1,32]{2,1,0:T(1,128)}, u32[]{:S(2)}) copy-start(s32[1,1,32]{2,1,0:T(1,128)} %rows.7) | copy-start | bytes 388
  2.9 46.7 %copy-start.5 = (s32[1,1,32]{2,1,0:T(1,128)S(1)}, s32[1,1,32]{2,1,0:T(1,128)}, u32[]{:S(2)}) copy-start(s32[1,1,32]{2,1,0:T(1,128)} %cols.7) | copy-start | bytes 388
  55.8 14.1 %copy-start.2 = (f32[64,128]{1,0:T(8,128)S(1)}, f32[64,128]{1,0:T(8,128)}, u32[]{:S(2)}) copy-start(f32[64,128]{1,0:T(8,128)} %h_ref.1) | copy-start | bytes 98308

commit v4 on v3

--- a/solution.py
+++ b/solution.py
@@ -1,5 +1,3 @@
-import functools
-
 import jax
 import jax.numpy as jnp
 from jax import lax
@@ -27,7 +25,6 @@
 bf16 = jnp.bfloat16
 VMEM = pl.BlockSpec(memory_space=pltpu.VMEM)
 SMEM = pl.BlockSpec(memory_space=pltpu.SMEM)
-HBM = pl.BlockSpec(memory_space=pltpu.HBM)
 
 
 def call(kernel, out_shape, in_specs, scratch=()):
@@ -35,7 +32,7 @@
         kernel,
         out_shape=out_shape,
         in_specs=in_specs,
-        out_specs=jax.tree.map(lambda _: VMEM, out_shape),
+        out_specs=jax.tree.map(lambda x: SMEM if x.dtype == jnp.int32 else VMEM, out_shape),
         scratch_shapes=scratch,
         compiler_params=pltpu.CompilerParams(vmem_limit_bytes=32 * 2**20),
     )
@@ -47,23 +44,22 @@
     return jnp.bitwise_and(lane, RANK - 1) == rank
 
 
-def start_kernel(count, w_any, h_any, own_ref, w_out, h_out, live_ref, w_ref, h_ref, sems):
-    w_copy = pltpu.make_async_copy(w_any, w_ref, sems.at[0])
-    h_copy = pltpu.make_async_copy(h_any, h_ref, sems.at[1])
-    w_copy.start()
-    h_copy.start()
+def start_h_kernel(h_ref, h_out):
+    h_half = h_ref[...].astype(bf16)
+    for k in range(N_CHIP):
+        h_out[k] = h_half
+
+
+def start_w_kernel(rows, cols, count, w_ref, own_ref, w_out, live_ref, place):
+    for g in range(CAP):
+        place[0, 0, g] = cols[0, 0, g] * ROW_TILES + rows[0, 0, g]
     slot = lax.broadcasted_iota(jnp.int32, (CAP, TILE), 0)
     live_ref[...] = (slot < count[0, 0]).astype(f32)
-    w_copy.wait()
     own_ref[:, :RANK] = w_ref[:OWN, :]
     own_ref[:, RANK:] = w_ref[OWN:, :]
     half = own_ref[...].astype(bf16)
     for k in range(N_KMER):
         w_out[k] = half
-    h_copy.wait()
-    h_half = h_ref[...].astype(bf16)
-    for k in range(N_CHIP):
-        h_out[k] = h_half
 
 
 def unpack(w_ref, tiles_ref):
@@ -74,8 +70,8 @@
         tiles_ref[r, 32 * q + OWN : 32 * q + 2 * OWN, :] = block[:, RANK:]
 
 
-def ratio_of(g, rows, cols, live_ref, values_ref, tiles_ref, h_ref):
-    r, c = rows[0, 0, g], cols[0, 0, g]
+def ratio_of(g, place, live_ref, values_ref, tiles_ref, h_ref):
+    r, c = place[0, 0, g] & (ROW_TILES - 1), place[0, 0, g] >> 2
     h_tile = h_ref[c & 1, c >> 1]
     estimate = jnp.dot(tiles_ref[r], h_tile, preferred_element_type=f32)
     ratio = values_ref[g].astype(f32) / estimate
@@ -83,7 +79,8 @@
     return r, c, h_tile, ratio
 
 
-def numer_h_kernel(rows, cols, live_ref, values_ref, w_ref, h_ref, out_ref, tiles_ref, flip_ref):
+def numer_h_kernel(place, live_ref, values_ref, w_ref, h_ref, out_ref, tiles_ref, flip_ref):
+    own_core = lax.axis_index("samp") & 1
     unpack(w_ref, tiles_ref)
     for r in range(ROW_TILES):
         flip_ref[r] = tiles_ref[r].T
@@ -91,8 +88,8 @@
     out_ref[:, :, :RANK, :] = jnp.zeros((2, N_CHIP, RANK, TILE), f32)
     out_ref[:, :, RANK:, :] = jnp.broadcast_to(sums[None, None], (2, N_CHIP, SUMS, TILE))
     for g in range(CAP):
-        r, c, h_tile, ratio = ratio_of(g, rows, cols, live_ref, values_ref, tiles_ref, h_ref)
-        out_ref[c & 1, c >> 1, :RANK, :] += jnp.dot(flip_ref[r], ratio, preferred_element_type=f32)
+        r, c, h_tile, ratio = ratio_of(g, place, live_ref, values_ref, tiles_ref, h_ref)
+        out_ref[jnp.bitwise_xor(c & 1, own_core), c >> 1, :RANK, :] += jnp.dot(flip_ref[r], ratio, preferred_element_type=f32)
 
 
 def update_h_kernel(parts_ref, h_ref, own_ref, out_ref):
@@ -107,7 +104,7 @@
         out_ref[k] = half
 
 
-def numer_w_kernel(rows, cols, live_ref, values_ref, w_ref, h_ref, out_ref, tiles_ref, acc_ref):
+def numer_w_kernel(place, live_ref, values_ref, w_ref, h_ref, out_ref, tiles_ref, acc_ref):
     unpack(w_ref, tiles_ref)
     sums = jnp.zeros((RANK, TILE), f32)
     for c in range(COL_TILES):
@@ -117,7 +114,7 @@
     out_ref[:, QUADS - 1] = jnp.broadcast_to(sums[None], (N_KMER, QUAD, TILE))
     acc_ref[...] = jnp.zeros_like(acc_ref)
     for g in range(CAP):
-        r, c, h_tile, ratio = ratio_of(g, rows, cols, live_ref, values_ref, tiles_ref, h_ref)
+        r, c, h_tile, ratio = ratio_of(g, place, live_ref, values_ref, tiles_ref, h_ref)
         acc_ref[r] += lax.dot_general(
             ratio, h_tile, (((1,), (1,)), ((), ())), preferred_element_type=f32
         )
@@ -150,6 +147,10 @@
     w_new = new_w(parts_ref, w_ref, rows_ref)
     own_ref[:OWN, :] = w_new[:, :RANK]
     own_ref[OWN:, :] = w_new[:, RANK:]
+
+
+def swap(bits):
+    return [(i, i ^ bits) for i in range(2 * N_CHIP)]
 
 
 def to_kmer(x):
@@ -174,27 +175,28 @@
     flip = pltpu.VMEM((ROW_TILES, RANK, TILE), bf16)
     acc = pltpu.VMEM((ROW_TILES, TILE, RANK), f32)
     rows = pltpu.VMEM((OWN, 2 * RANK), f32)
-    fetched = [pltpu.VMEM(w_init.shape, f32), pltpu.VMEM(h_init.shape, f32), pltpu.SemaphoreType.DMA((2,))]
-    wide = [SMEM] * 2 + [VMEM] * 4
+    wide = [SMEM] + [VMEM] * 4
 
     live = shape((CAP, TILE), f32)
-    start = call(start_kernel, (w_own, w_spread, h_spread, live), [SMEM] + [HBM] * 2, fetched)
+    start_h = call(start_h_kernel, h_spread, [VMEM])
+    place = shape((1, 1, CAP), jnp.int32)
+    start_w = call(start_w_kernel, (w_own, w_spread, live, place), [SMEM] * 3 + [VMEM])
     numer_h = call(numer_h_kernel, shape((2, N_CHIP, RANK + SUMS, TILE), f32), wide, [tiles, flip])
     update_h = call(update_h_kernel, (h_own, h_spread), [VMEM] * 2)
     numer_w = call(numer_w_kernel, shape((N_KMER, QUADS, QUAD, TILE), f32), wide, [tiles, acc])
     update_w = call(update_w_kernel, (w_own, w_spread), [VMEM] * 2, [rows])
     last_w = call(last_w_kernel, shape((2 * OWN, RANK), f32), [VMEM] * 2, [rows])
 
-    w_own, w_out, h_out, live = start(tile_count, w_init, h_init)
-    slots = (tile_rows, tile_cols, live)
+    h_out = start_h(h_init)
+    w_own, w_out, live, place = start_w(tile_rows, tile_cols, tile_count, w_init)
+    slots = (place, live)
     h_own = h_init
     w_panel = to_kmer(w_out)
-    w_panel, h_out = lax.optimization_barrier((w_panel, h_out))
     h_panel = panel_of(h_out)
     for sweep in range(ITERS):
         numer = numer_h(*slots, values, w_panel, h_panel)
-        halves = lax.all_to_all(numer, "samp", 0, 0, axis_index_groups=CORES)
-        h_own, h_out = update_h(to_chips(halves[0] + halves[1]), h_own)
+        numer = numer[0] + lax.ppermute(numer[1], "samp", swap(1))
+        h_own, h_out = update_h(to_chips(numer), h_own)
         h_panel = panel_of(h_out)
         parts = to_kmer(numer_w(*slots, values, w_panel, h_panel))
         if sweep < ITERS - 1:

time: 179 us -> 175 us (0.978)
  blocking collectives: 165 us -> 112 us
  starting transfers between devices: 0 us -> 32 us
  waiting for transfers between devices: 0 us -> 14.4 us
    all_to_all x4 -> x3, blocking collectives: 75.8 us -> 48.6 us  [to_kmer(): return lax.all_to_all(x, 'kmer', 0, 0)]
    all_to_all x0 -> x2, starting transfers between devices: none -> 22.4 us  [the longest x1 14.8 us: to_kmer(): return lax.all_to_all(x, 'kmer', 0, 0)]
    all_to_all x5 -> x4, blocking collectives: 64 us -> 49.8 us  [to_chips(): return lax.all_to_all(x, 'samp', 0, 0, axis_index_groups=CHIPS)]
    all_to_all x2 -> x0, blocking collectives: 11.2 us -> none  [body(): halves = lax.all_to_all(numer, 'samp', 0, 0, axis_index_groups=CORES)]
    all_to_all x0 -> x2, waiting for transfers between devices: none -> 11.2 us  [the longest x1 7.47 us: to_kmer(): return lax.all_to_all(x, 'kmer', 0, 0)]
    ppermute x0 -> x2, starting transfers between devices: none -> 9.59 us  [body(): numer = numer[0] + lax.ppermute(numer[1], 'samp', swap(1))]
    ppermute x0 -> x2, waiting for transfers between devices: none -> 3.22 us  [body(): numer = numer[0] + lax.ppermute(numer[1], 'samp', swap(1))]
    pallas_call x3 -> x4, Pallas kernels: 1.04 us -> 2.84 us  [the longest x1 1.25 us: body(): start_w(tile_rows, tile_cols, tile_count, w_init)]
  transfers between devices with their start and end apart: 0 -> 4, of which waited for: 0 -> 4; matrix products, arithmetic and copies ran while one was open for 0% -> 0% of each run, Pallas kernels for 0% -> 1%
where the time goes in v4:
time: 175 us; the launch traced here: 172 us
  blocking collectives  112 us (64%)
  starting transfers between devices  32 us (18%)
  waiting for transfers between devices  14.4 us (8%)
  Pallas kernels  9.68 us (6%)
  local copies, waits for them, and re-layouts  2.87 us (2%)
    all_to_all x4, blocking collectives, to_chips(): return lax.all_to_all(x, 'samp', 0, 0, axis_index_groups=CHIPS)  49.8 us
    all_to_all x3, blocking collectives, to_kmer(): return lax.all_to_all(x, 'kmer', 0, 0)  48.6 us
    all_to_all x1, starting transfers between devices, to_kmer(): return lax.all_to_all(x, 'kmer', 0, 0)  14.8 us
    all_gather x3, blocking collectives, panel_of(): lax.all_gather(to_chips(spread), 'samp', axis=0, axis_index_groups=CORES)  13.2 us
    ppermute x2, starting transfers between devices, body(): numer = numer[0] + lax.ppermute(numer[1], 'samp', swap(1))  9.59 us
    all_to_all x1, starting transfers between devices, to_chips(): return lax.all_to_all(x, 'samp', 0, 0, axis_index_groups=CHIPS)  7.58 us
    all_to_all x1, waiting for transfers between devices, to_kmer(): return lax.all_to_all(x, 'kmer', 0, 0)  7.47 us
    all_to_all x1, waiting for transfers between devices, to_chips(): return lax.all_to_all(x, 'samp', 0, 0, axis_index_groups=CHIPS)  3.73 us
  transfers between devices with their start and end apart: 4, of which 4 were waited for; matrix products, arithmetic and copies ran while one was open for 0% of the time, Pallas kernels for 1%

profile of v4, /device:TPU:1, one launch (start us, length us, event | category | flops | bytes accessed | tf_op | source)
XLA Modules:
  0.0 172.1 jit_solution(4180792780071273571)
XLA Ops:
  0.6 0.7 copy-done.1
  1.4 0.7 shard_map.78
  2.1 7.6 %all-to-all-start.1 = ((bf16[16,64,128]{2,1,0:T(8,128)(2,1)}), bf16[16,64,128]{2,1,0:T(8,128)(2,1)S(1)}, u32[]{:S(2)}, u32[]{:S(2)}) async-start(bf16[16,64,128]{2,1,0:T(8,128)(2,1)} %shard_map.78), calls=%async_computation.1 | async-start | bytes 524288 | tf_op jit(solution)/shard_map/all_to_all | solution.py:161
  10.4 0.7 copy-done.3
  11.1 0.7 copy-done.4
  11.7 0.7 copy-done.5
  12.4 1.3 shard_map.77
  13.7 3.7 %all-to-all-done.1 = bf16[16,64,128]{2,1,0:T(8,128)(2,1)S(1)} async-done(((bf16[16,64,128]{2,1,0:T(8,128)(2,1)}), bf16[16,64,128]{2,1,0:T(8,128)(2,1)S(1)}, u32[]{:S(2)}, u32[]{:S(2)}) %all-to-all-start.1) | async-done | bytes 262176 | tf_op jit(solution)/shard_map/all_to_all | solution.py:161
  17.4 14.8 %all-to-all-start = ((bf16[16,16,128]{2,1,0:T(8,128)(2,1)}), bf16[16,16,128]{2,1,0:T(8,128)(2,1)S(1)}, u32[]{:S(2)}, u32[]{:S(2)}) async-start(bf16[16,16,128]{2,1,0:T(8,128)(2,1)} %get-tuple-element.14), calls=%async_computation | async-start | bytes 131072 | tf_op jit(solution)/shard_map/all_to_all | solution.py:157
  32.2 4.2 %all-gather = bf16[32,64,128]{2,1,0:T(8,128)(2,1)S(1)} all-gather(bf16[16,64,128]{2,1,0:T(8,128)(2,1)S(1)} %all-to-all-done.1), channel_id=2, replica_groups={{0,16},{32,48},{64,80},{96,112},{128,144},{160,176},{192,208},{224,240}..., dimensions={0}, use_global_device_ids=true | all-gather | bytes 786432 | tf_op jit(solution)/shard_map/all_gather | solution.py:165
  36.4 7.5 %all-to-all-done.w_ref = bf16[16,16,128]{2,1,0:T(8,128)(2,1)S(1)} async-done(((bf16[16,16,128]{2,1,0:T(8,128)(2,1)}), bf16[16,16,128]{2,1,0:T(8,128)(2,1)S(1)}, u32[]{:S(2)}, u32[]{:S(2)}) %all-to-all-start) | async-done | bytes 65568 | tf_op jit(solution)/shard_map/all_to_all | solution.py:157
  43.8 1.5 shard_map.79
  45.4 5.4 %collective-permute-start = (f32[16,72,128]{2,1,0:T(8,128)S(1)}, f32[16,72,128]{2,1,0:T(8,128)S(1)}, u32[]{:S(2)}, u32[]{:S(2)}) collective-permute-start(f32[16,72,128]{2,1,0:T(8,128)S(1)} %slice_bitcast_fusion.2), channel_id=1, source_target_pairs={{0,16},{16,0},{32,48},{48,32},{64,80},{80,64},{96,112},{112,96},{1... | collective-permute-start | bytes 1769480 | tf_op jit(solution)/shard_map/ppermute | solution.py:198
  50.9 1.6 collective-permute-done
  52.5 0.1 fusion.1
  52.5 14.0 %all_to_all.45.parts_ref = f32[16,72,128]{2,1,0:T(8,128)S(1)} all-to-all(f32[16,72,128]{2,1,0:T(8,128)S(1)} %fusion.1), channel_id=1, replica_groups={{0,32,64,96,128,160,192,224,256,288,320,352,384,416,448,480},{16,48,80,..., dimensions={0} | all-to-all | bytes 1179648 | tf_op jit(solution)/shard_map/all_to_all | solution.py:161
  66.5 0.1 shard_map.80
  66.7 10.9 %all_to_all.46 = bf16[16,64,128]{2,1,0:T(8,128)(2,1)S(1)} all-to-all(bf16[16,64,128]{2,1,0:T(8,128)(2,1)S(1)} %get-tuple-element.15), channel_id=1, replica_groups={{0,32,64,96,128,160,192,224,256,288,320,352,384,416,448,480},{16,48,80,..., dimensions={0} | all-to-all | bytes 524288 | tf_op jit(solution)/shard_map/all_to_all | solution.py:161
  77.6 4.5 %all-gather.1 = bf16[32,64,128]{2,1,0:T(8,128)(2,1)S(1)} all-gather(bf16[16,64,128]{2,1,0:T(8,128)(2,1)S(1)} %all_to_all.46), channel_id=3, replica_groups={{0,16},{32,48},{64,80},{96,112},{128,144},{160,176},{192,208},{224,240}..., dimensions={0}, use_global_device_ids=true | all-gather | bytes 786432 | tf_op jit(solution)/shard_map/all_gather | solution.py:165
  82.1 1.6 shard_map.81
  83.7 14.9 %all_to_all.47.parts_ref = f32[16,5,4,128]{3,2,1,0:T(4,128)S(1)} all-to-all(f32[16,5,4,128]{3,2,1,0:T(4,128)S(1)} %shard_map.81), channel_id=1, replica_groups=mesh['samp'=32,'kmer'=16] {'kmer'}, dimensions={0} | all-to-all | bytes 327680 | tf_op jit(solution)/shard_map/all_to_all | solution.py:157
  98.6 18.9 %all_to_all.48.w_ref = bf16[16,16,128]{2,1,0:T(8,128)(2,1)S(1)} all-to-all(bf16[16,16,128]{2,1,0:T(8,128)(2,1)S(1)} %get-tuple-element.17), channel_id=1, replica_groups=mesh['samp'=32,'kmer'=16] {'kmer'}, dimensions={0} | all-to-all | bytes 131072 | tf_op jit(solution)/shard_map/all_to_all | solution.py:157
  117.4 1.5 shard_map.83
  119.0 4.1 %collective-permute-start.1 = (f32[16,72,128]{2,1,0:T(8,128)S(1)}, f32[16,72,128]{2,1,0:T(8,128)S(1)}, u32[]{:S(2)}, u32[]{:S(2)}) collective-permute-start(f32[16,72,128]{2,1,0:T(8,128)S(1)} %slice_bitcast_fusion), channel_id=1, source_target_pairs={{0,16},{16,0},{32,48},{48,32},{64,80},{80,64},{96,112},{112,96},{1... | collective-permute-start | bytes 1769480 | tf_op jit(solution)/shard_map/ppermute | solution.py:198
  123.1 1.6 collective-permute-done.1
  124.8 14.0 %all_to_all.49.parts_ref = f32[16,72,128]{2,1,0:T(8,128)S(1)} all-to-all(f32[16,72,128]{2,1,0:T(8,128)S(1)} %fusion), channel_id=1, replica_groups={{0,32,64,96,128,160,192,224,256,288,320,352,384,416,448,480},{16,48,80,..., dimensions={0} | all-to-all | bytes 1179648 | tf_op jit(solution)/shard_map/all_to_all | solution.py:161
  138.8 0.7 shard_map.84
  139.6 10.9 %all_to_all.50 = bf16[16,64,128]{2,1,0:T(8,128)(2,1)S(1)} all-to-all(bf16[16,64,128]{2,1,0:T(8,128)(2,1)S(1)} %get-tuple-element.19), channel_id=1, replica_groups={{0,32,64,96,128,160,192,224,256,288,320,352,384,416,448,480},{16,48,80,..., dimensions={0} | all-to-all | bytes 524288 | tf_op jit(solution)/shard_map/all_to_all | solution.py:161
  150.5 4.5 %all-gather.2 = bf16[32,64,128]{2,1,0:T(8,128)(2,1)S(1)} all-gather(bf16[16,64,128]{2,1,0:T(8,128)(2,1)S(1)} %all_to_all.50), channel_id=4, replica_groups={{0,16},{32,48},{64,80},{96,112},{128,144},{160,176},{192,208},{224,240}..., dimensions={0}, use_global_device_ids=true | all-gather | bytes 786432 | tf_op jit(solution)/shard_map/all_gather | solution.py:165
  155.0 1.6 shard_map.85
  156.6 14.9 %all_to_all.51.parts_ref = f32[16,5,4,128]{3,2,1,0:T(4,128)S(1)} all-to-all(f32[16,5,4,128]{3,2,1,0:T(4,128)S(1)} %shard_map.85), channel_id=1, replica_groups=mesh['samp'=32,'kmer'=16] {'kmer'}, dimensions={0} | all-to-all | bytes 327680 | tf_op jit(solution)/shard_map/all_to_all | solution.py:157
  171.4 0.7 shard_map.86
  (12 shorter events, 0.2 us)
Async XLA Ops:
  0.6 0.8 copy-start.1
  1.4 42.5 %copy-start = (bf16[1,1,32,128,128]{4,3,2,1,0:T(8,128)(2,1)S(1)}, bf16[1,1,32,128,128]{4,3,2,1,0:T(8,128)(2,1)}, u32[]{:S(2)}) copy-start(bf16[1,1,32,128,128]{4,3,2,1,0:T(8,128)(2,1)} %param.9) | copy-start | bytes 3145732
  2.1 15.3 %all-to-all-start.1 = ((bf16[16,64,128]{2,1,0:T(8,128)(2,1)}), bf16[16,64,128]{2,1,0:T(8,128)(2,1)S(1)}, u32[]{:S(2)}, u32[]{:S(2)}) async-start(bf16[16,64,128]{2,1,0:T(8,128)(2,1)} %shard_map.78), calls=%async_computation.1 | async-start | bytes 524288 | tf_op jit(solution)/shard_map/all_to_all | solution.py:161
  10.4 0.7 copy-start.3
  11.1 0.7 copy-start.4
  11.7 0.7 copy-start.5
  17.4 26.5 %all-to-all-start = ((bf16[16,16,128]{2,1,0:T(8,128)(2,1)}), bf16[16,16,128]{2,1,0:T(8,128)(2,1)S(1)}, u32[]{:S(2)}, u32[]{:S(2)}) async-start(bf16[16,16,128]{2,1,0:T(8,128)(2,1)} %get-tuple-element.14), calls=%async_computation | async-start | bytes 131072 | tf_op jit(solution)/shard_map/all_to_all | solution.py:157
  45.4 21.1 %copy-start.2 = (f32[64,128]{1,0:T(8,128)S(1)}, f32[64,128]{1,0:T(8,128)}, u32[]{:S(2)}) copy-start(f32[64,128]{1,0:T(8,128)} %h_ref.3) | copy-start | bytes 98308
  45.4 7.1 %collective-permute-start = (f32[16,72,128]{2,1,0:T(8,128)S(1)}, f32[16,72,128]{2,1,0:T(8,128)S(1)}, u32[]{:S(2)}, u32[]{:S(2)}) collective-permute-start(f32[16,72,128]{2,1,0:T(8,128)S(1)} %slice_bitcast_fusion.2), channel_id=1, source_target_pairs={{0,16},{16,0},{32,48},{48,32},{64,80},{80,64},{96,112},{112,96},{1... | collective-permute-start | bytes 1769480 | tf_op jit(solution)/shard_map/ppermute | solution.py:198
  119.0 5.8 %collective-permute-start.1 = (f32[16,72,128]{2,1,0:T(8,128)S(1)}, f32[16,72,128]{2,1,0:T(8,128)S(1)}, u32[]{:S(2)}, u32[]{:S(2)}) collective-permute-start(f32[16,72,128]{2,1,0:T(8,128)S(1)} %slice_bitcast_fusion), channel_id=1, source_target_pairs={{0,16},{16,0},{32,48},{48,32},{64,80},{80,64},{96,112},{112,96},{1... | collective-permute-start | bytes 1769480 | tf_op jit(solution)/shard_map/ppermute | solution.py:198

commit v5 on v4

--- a/solution.py
+++ b/solution.py
@@ -15,8 +15,7 @@
 N_CHIP = 16
 OWN = 16
 SUMS = 8
-QUAD = 4
-QUADS = OWN // QUAD + 1
+ROWS = OWN + 1
 
 CORES = [[2 * a, 2 * a + 1] for a in range(N_CHIP)]
 CHIPS = [[2 * a + c for a in range(N_CHIP)] for c in range(2)]
@@ -27,12 +26,12 @@
 SMEM = pl.BlockSpec(memory_space=pltpu.SMEM)
 
 
-def call(kernel, out_shape, in_specs, scratch=()):
+def call(kernel, out_shape, in_specs, scratch=(), out_spec=VMEM):
     return pl.pallas_call(
         kernel,
         out_shape=out_shape,
         in_specs=in_specs,
-        out_specs=jax.tree.map(lambda x: SMEM if x.dtype == jnp.int32 else VMEM, out_shape),
+        out_specs=jax.tree.map(lambda x: SMEM if x.dtype == jnp.int32 else out_spec, out_shape),
         scratch_shapes=scratch,
         compiler_params=pltpu.CompilerParams(vmem_limit_bytes=32 * 2**20),
     )
@@ -70,6 +69,12 @@
         tiles_ref[r, 32 * q + OWN : 32 * q + 2 * OWN, :] = block[:, RANK:]
 
 
+def fetch(place_ref, place, sem):
+    copy = pltpu.make_async_copy(place_ref, place, sem)
+    copy.start()
+    return copy
+
+
 def ratio_of(g, place, live_ref, values_ref, tiles_ref, h_ref):
     r, c = place[0, 0, g] & (ROW_TILES - 1), place[0, 0, g] >> 2
     h_tile = h_ref[c & 1, c >> 1]
@@ -79,7 +84,8 @@
     return r, c, h_tile, ratio
 
 
-def numer_h_kernel(place, live_ref, values_ref, w_ref, h_ref, out_ref, tiles_ref, flip_ref):
+def numer_h_kernel(place_ref, live_ref, values_ref, w_ref, h_ref, out_ref, place, sem, tiles_ref, flip_ref):
+    copy = fetch(place_ref, place, sem)
     own_core = lax.axis_index("samp") & 1
     unpack(w_ref, tiles_ref)
     for r in range(ROW_TILES):
@@ -87,6 +93,7 @@
     sums = jnp.sum(w_ref[...].astype(f32).reshape(N_KMER * OWN, 2 * RANK), axis=0, keepdims=True)
     out_ref[:, :, :RANK, :] = jnp.zeros((2, N_CHIP, RANK, TILE), f32)
     out_ref[:, :, RANK:, :] = jnp.broadcast_to(sums[None, None], (2, N_CHIP, SUMS, TILE))
+    copy.wait()
     for g in range(CAP):
         r, c, h_tile, ratio = ratio_of(g, place, live_ref, values_ref, tiles_ref, h_ref)
         out_ref[jnp.bitwise_xor(c & 1, own_core), c >> 1, :RANK, :] += jnp.dot(flip_ref[r], ratio, preferred_element_type=f32)
@@ -104,15 +111,16 @@
         out_ref[k] = half
 
 
-def numer_w_kernel(place, live_ref, values_ref, w_ref, h_ref, out_ref, tiles_ref, acc_ref):
+def numer_w_kernel(place_ref, live_ref, values_ref, w_ref, h_ref, out_ref, place, sem, tiles_ref, acc_ref):
+    copy = fetch(place_ref, place, sem)
     unpack(w_ref, tiles_ref)
     sums = jnp.zeros((RANK, TILE), f32)
     for c in range(COL_TILES):
         sums = sums + h_ref[c % 2, c // 2].astype(f32)
     sums = jnp.where(same_rank((RANK, TILE)), jnp.sum(sums, axis=1, keepdims=True), 0.0)
     sums = jnp.sum(sums, axis=0, keepdims=True)
-    out_ref[:, QUADS - 1] = jnp.broadcast_to(sums[None], (N_KMER, QUAD, TILE))
     acc_ref[...] = jnp.zeros_like(acc_ref)
+    copy.wait()
     for g in range(CAP):
         r, c, h_tile, ratio = ratio_of(g, place, live_ref, values_ref, tiles_ref, h_ref)
         acc_ref[r] += lax.dot_general(
@@ -120,33 +128,38 @@
         )
     for k in range(N_KMER):
         r, q = k // 4, k % 4
-        for a in range(OWN // QUAD):
-            row = 32 * q + QUAD * a
-            out_ref[k, a, :, :RANK] = acc_ref[r, row : row + QUAD, :]
-            out_ref[k, a, :, RANK:] = acc_ref[r, row + OWN : row + OWN + QUAD, :]
-
-
-def new_w(parts_ref, w_ref, rows_ref):
-    summed = parts_ref[0]
+        out_ref[k * ROWS : k * ROWS + OWN, :RANK] = acc_ref[r, 32 * q : 32 * q + OWN, :]
+        out_ref[k * ROWS : k * ROWS + OWN, RANK:] = acc_ref[r, 32 * q + OWN : 32 * q + 2 * OWN, :]
+        out_ref[k * ROWS + OWN : (k + 1) * ROWS, :] = sums
+
+
+def new_w(parts_ref, w_ref):
+    summed = parts_ref[:OWN, :]
+    total = parts_ref[OWN:ROWS, :]
     for k in range(1, N_KMER):
-        summed = summed + parts_ref[k]
-    for a in range(OWN // QUAD):
-        rows_ref[QUAD * a : QUAD * a + QUAD, :] = summed[a]
-    return w_ref[...] * rows_ref[...] / summed[QUADS - 1, :1]
-
-
-def update_w_kernel(parts_ref, w_ref, own_ref, out_ref, rows_ref):
-    w_new = new_w(parts_ref, w_ref, rows_ref)
+        summed = summed + parts_ref[k * ROWS : k * ROWS + OWN, :]
+        total = total + parts_ref[k * ROWS + OWN : (k + 1) * ROWS, :]
+    return w_ref[...] * summed / total
+
+
+def update_w_kernel(parts_ref, w_ref, own_ref, out_ref):
+    w_new = new_w(parts_ref, w_ref)
     own_ref[...] = w_new
     half = w_new.astype(bf16)
     for k in range(N_KMER):
         out_ref[k] = half
 
 
-def last_w_kernel(parts_ref, w_ref, own_ref, rows_ref):
-    w_new = new_w(parts_ref, w_ref, rows_ref)
+def last_w_kernel(parts_ref, w_ref, h_ref, w_out, h_out, own_ref, sems):
+    h_copy = pltpu.make_async_copy(h_ref, h_out, sems.at[0])
+    h_copy.start()
+    w_new = new_w(parts_ref, w_ref)
     own_ref[:OWN, :] = w_new[:, :RANK]
     own_ref[OWN:, :] = w_new[:, RANK:]
+    w_copy = pltpu.make_async_copy(own_ref, w_out, sems.at[1])
+    w_copy.start()
+    h_copy.wait()
+    w_copy.wait()
 
 
 def swap(bits):
@@ -174,18 +187,24 @@
     tiles = pltpu.VMEM((ROW_TILES, TILE, RANK), bf16)
     flip = pltpu.VMEM((ROW_TILES, RANK, TILE), bf16)
     acc = pltpu.VMEM((ROW_TILES, TILE, RANK), f32)
-    rows = pltpu.VMEM((OWN, 2 * RANK), f32)
-    wide = [SMEM] + [VMEM] * 4
+    wide = [VMEM] * 5
+    fetched = [pltpu.SMEM((1, 1, CAP), jnp.int32), pltpu.SemaphoreType.DMA(())]
 
     live = shape((CAP, TILE), f32)
     start_h = call(start_h_kernel, h_spread, [VMEM])
     place = shape((1, 1, CAP), jnp.int32)
     start_w = call(start_w_kernel, (w_own, w_spread, live, place), [SMEM] * 3 + [VMEM])
-    numer_h = call(numer_h_kernel, shape((2, N_CHIP, RANK + SUMS, TILE), f32), wide, [tiles, flip])
+    numer_h = call(numer_h_kernel, shape((2, N_CHIP, RANK + SUMS, TILE), f32), wide, fetched + [tiles, flip])
     update_h = call(update_h_kernel, (h_own, h_spread), [VMEM] * 2)
-    numer_w = call(numer_w_kernel, shape((N_KMER, QUADS, QUAD, TILE), f32), wide, [tiles, acc])
-    update_w = call(update_w_kernel, (w_own, w_spread), [VMEM] * 2, [rows])
-    last_w = call(last_w_kernel, shape((2 * OWN, RANK), f32), [VMEM] * 2, [rows])
+    numer_w = call(numer_w_kernel, shape((N_KMER * ROWS, TILE), f32), wide, fetched + [tiles, acc])
+    update_w = call(update_w_kernel, (w_own, w_spread), [VMEM] * 2)
+    last_w = call(
+        last_w_kernel,
+        (shape(w_init.shape, f32), shape(h_init.shape, f32)),
+        [VMEM] * 3,
+        [pltpu.VMEM(w_init.shape, f32), pltpu.SemaphoreType.DMA((2,))],
+        pl.BlockSpec(memory_space=pl.ANY),
+    )
 
     h_out = start_h(h_init)
     w_own, w_out, live, place = start_w(tile_rows, tile_cols, tile_count, w_init)
@@ -198,11 +217,12 @@
         numer = numer[0] + lax.ppermute(numer[1], "samp", swap(1))
         h_own, h_out = update_h(to_chips(numer), h_own)
         h_panel = panel_of(h_out)
-        parts = to_kmer(numer_w(*slots, values, w_panel, h_panel))
+        parts = numer_w(*slots, values, w_panel, h_panel).reshape(N_KMER, ROWS, 1, TILE)
+        parts = to_kmer(parts).reshape(N_KMER * ROWS, TILE)
         if sweep < ITERS - 1:
             w_own, w_out = update_w(parts, w_own)
             w_panel = to_kmer(w_out)
-    return last_w(parts, w_own), h_own
+    return last_w(parts, w_own, h_own)
 
 
 def solution(mesh):

time: 175 us -> 172 us (0.983)
  no operation moved by 1% of the time
where the time goes in v5:
time: 172 us; the launch traced here: 170 us
  blocking collectives  111 us (65%)
  starting transfers between devices  31.9 us (19%)
  waiting for transfers between devices  14.4 us (8%)
  Pallas kernels  8.74 us (5%)
  local copies, waits for them, and re-layouts  2.87 us (2%)
    all_to_all x4, blocking collectives, to_chips(): return lax.all_to_all(x, 'samp', 0, 0, axis_index_groups=CHIPS)  49.9 us
    all_to_all x3, blocking collectives, to_kmer(): return lax.all_to_all(x, 'kmer', 0, 0)  47.5 us
    all_to_all x1, starting transfers between devices, to_kmer(): return lax.all_to_all(x, 'kmer', 0, 0)  14.8 us
    all_gather x3, blocking collectives, panel_of(): lax.all_gather(to_chips(spread), 'samp', axis=0, axis_index_groups=CORES)  13.2 us
    ppermute x2, starting transfers between devices, body(): numer = numer[0] + lax.ppermute(numer[1], 'samp', swap(1))  9.53 us
    all_to_all x1, starting transfers between devices, to_chips(): return lax.all_to_all(x, 'samp', 0, 0, axis_index_groups=CHIPS)  7.58 us
    all_to_all x1, waiting for transfers between devices, to_kmer(): return lax.all_to_all(x, 'kmer', 0, 0)  7.47 us
    all_to_all x1, waiting for transfers between devices, to_chips(): return lax.all_to_all(x, 'samp', 0, 0, axis_index_groups=CHIPS)  3.73 us
  transfers between devices with their start and end apart: 4, of which 4 were waited for; matrix products, arithmetic and copies ran while one was open for 0% of the time, Pallas kernels for 1%

profile of v5, /device:TPU:1, one launch (start us, length us, event | category | flops | bytes accessed | tf_op | source)
XLA Modules:
  0.0 170.1 jit_solution(17703562443748000956)
XLA Ops:
  0.6 0.7 copy-done.1
  1.4 0.7 shard_map.78
  2.1 7.6 %all-to-all-start.1 = ((bf16[16,64,128]{2,1,0:T(8,128)(2,1)}), bf16[16,64,128]{2,1,0:T(8,128)(2,1)S(1)}, u32[]{:S(2)}, u32[]{:S(2)}) async-start(bf16[16,64,128]{2,1,0:T(8,128)(2,1)} %shard_map.78), calls=%async_computation.1 | async-start | bytes 524288 | tf_op jit(solution)/shard_map/all_to_all | solution.py:174
  10.4 0.7 copy-done.3
  11.1 0.7 copy-done.4
  11.7 0.7 copy-done.5
  12.4 1.3 shard_map.77
  13.7 3.7 %all-to-all-done.1 = bf16[16,64,128]{2,1,0:T(8,128)(2,1)S(1)} async-done(((bf16[16,64,128]{2,1,0:T(8,128)(2,1)}), bf16[16,64,128]{2,1,0:T(8,128)(2,1)S(1)}, u32[]{:S(2)}, u32[]{:S(2)}) %all-to-all-start.1) | async-done | bytes 262176 | tf_op jit(solution)/shard_map/all_to_all | solution.py:174
  17.4 14.8 %all-to-all-start = ((bf16[16,16,128]{2,1,0:T(8,128)(2,1)}), bf16[16,16,128]{2,1,0:T(8,128)(2,1)S(1)}, u32[]{:S(2)}, u32[]{:S(2)}) async-start(bf16[16,16,128]{2,1,0:T(8,128)(2,1)} %get-tuple-element.14), calls=%async_computation | async-start | bytes 131072 | tf_op jit(solution)/shard_map/all_to_all | solution.py:170
  32.2 4.2 %all-gather = bf16[32,64,128]{2,1,0:T(8,128)(2,1)S(1)} all-gather(bf16[16,64,128]{2,1,0:T(8,128)(2,1)S(1)} %all-to-all-done.1), channel_id=2, replica_groups={{0,16},{32,48},{64,80},{96,112},{128,144},{160,176},{192,208},{224,240}..., dimensions={0}, use_global_device_ids=true | all-gather | bytes 786432 | tf_op jit(solution)/shard_map/all_gather | solution.py:178
  36.4 7.5 %all-to-all-done.w_ref = bf16[16,16,128]{2,1,0:T(8,128)(2,1)S(1)} async-done(((bf16[16,16,128]{2,1,0:T(8,128)(2,1)}), bf16[16,16,128]{2,1,0:T(8,128)(2,1)S(1)}, u32[]{:S(2)}, u32[]{:S(2)}) %all-to-all-start) | async-done | bytes 65568 | tf_op jit(solution)/shard_map/all_to_all | solution.py:170
  43.8 1.4 shard_map.79
  45.3 5.5 %collective-permute-start = (f32[16,72,128]{2,1,0:T(8,128)S(1)}, f32[16,72,128]{2,1,0:T(8,128)S(1)}, u32[]{:S(2)}, u32[]{:S(2)}) collective-permute-start(f32[16,72,128]{2,1,0:T(8,128)S(1)} %slice_bitcast_fusion.2), channel_id=1, source_target_pairs={{0,16},{16,0},{32,48},{48,32},{64,80},{80,64},{96,112},{112,96},{1... | collective-permute-start | bytes 1769480 | tf_op jit(solution)/shard_map/ppermute | solution.py:217
  50.7 1.6 collective-permute-done
  52.4 14.0 %all_to_all.45.parts_ref = f32[16,72,128]{2,1,0:T(8,128)S(1)} all-to-all(f32[16,72,128]{2,1,0:T(8,128)S(1)} %fusion.1), channel_id=1, replica_groups={{0,32,64,96,128,160,192,224,256,288,320,352,384,416,448,480},{16,48,80,..., dimensions={0} | all-to-all | bytes 1179648 | tf_op jit(solution)/shard_map/all_to_all | solution.py:174
  66.4 0.1 shard_map.80
  66.6 10.9 %all_to_all.46 = bf16[16,64,128]{2,1,0:T(8,128)(2,1)S(1)} all-to-all(bf16[16,64,128]{2,1,0:T(8,128)(2,1)S(1)} %get-tuple-element.15), channel_id=1, replica_groups={{0,32,64,96,128,160,192,224,256,288,320,352,384,416,448,480},{16,48,80,..., dimensions={0} | all-to-all | bytes 524288 | tf_op jit(solution)/shard_map/all_to_all | solution.py:174
  77.5 4.5 %all-gather.1 = bf16[32,64,128]{2,1,0:T(8,128)(2,1)S(1)} all-gather(bf16[16,64,128]{2,1,0:T(8,128)(2,1)S(1)} %all_to_all.46), channel_id=3, replica_groups={{0,16},{32,48},{64,80},{96,112},{128,144},{160,176},{192,208},{224,240}..., dimensions={0}, use_global_device_ids=true | all-gather | bytes 786432 | tf_op jit(solution)/shard_map/all_gather | solution.py:178
  82.0 1.5 shard_map.81
  83.5 14.7 %all_to_all.47 = f32[16,17,1,128]{3,2,1,0:T(1,128)S(1)} all-to-all(f32[16,17,1,128]{3,2,1,0:T(1,128)S(1)} %bitcast.31), channel_id=1, replica_groups=mesh['samp'=32,'kmer'=16] {'kmer'}, dimensions={0} | all-to-all | bytes 278528 | tf_op jit(solution)/shard_map/all_to_all | solution.py:170
  98.2 18.1 %all_to_all.48.w_ref = bf16[16,16,128]{2,1,0:T(8,128)(2,1)S(1)} all-to-all(bf16[16,16,128]{2,1,0:T(8,128)(2,1)S(1)} %get-tuple-element.17), channel_id=1, replica_groups=mesh['samp'=32,'kmer'=16] {'kmer'}, dimensions={0} | all-to-all | bytes 131072 | tf_op jit(solution)/shard_map/all_to_all | solution.py:170
  116.3 1.4 shard_map.83
  117.7 4.1 %collective-permute-start.1 = (f32[16,72,128]{2,1,0:T(8,128)S(1)}, f32[16,72,128]{2,1,0:T(8,128)S(1)}, u32[]{:S(2)}, u32[]{:S(2)}) collective-permute-start(f32[16,72,128]{2,1,0:T(8,128)S(1)} %slice_bitcast_fusion), channel_id=1, source_target_pairs={{0,16},{16,0},{32,48},{48,32},{64,80},{80,64},{96,112},{112,96},{1... | collective-permute-start | bytes 1769480 | tf_op jit(solution)/shard_map/ppermute | solution.py:217
  121.8 1.6 collective-permute-done.1
  123.4 0.1 fusion
  123.5 14.0 %all_to_all.49.parts_ref = f32[16,72,128]{2,1,0:T(8,128)S(1)} all-to-all(f32[16,72,128]{2,1,0:T(8,128)S(1)} %fusion), channel_id=1, replica_groups={{0,32,64,96,128,160,192,224,256,288,320,352,384,416,448,480},{16,48,80,..., dimensions={0} | all-to-all | bytes 1179648 | tf_op jit(solution)/shard_map/all_to_all | solution.py:174
  137.5 0.1 shard_map.84
  137.7 10.9 %all_to_all.50 = bf16[16,64,128]{2,1,0:T(8,128)(2,1)S(1)} all-to-all(bf16[16,64,128]{2,1,0:T(8,128)(2,1)S(1)} %get-tuple-element.19), channel_id=1, replica_groups={{0,32,64,96,128,160,192,224,256,288,320,352,384,416,448,480},{16,48,80,..., dimensions={0} | all-to-all | bytes 524288 | tf_op jit(solution)/shard_map/all_to_all | solution.py:174
  148.6 4.5 %all-gather.2 = bf16[32,64,128]{2,1,0:T(8,128)(2,1)S(1)} all-gather(bf16[16,64,128]{2,1,0:T(8,128)(2,1)S(1)} %all_to_all.50), channel_id=4, replica_groups={{0,16},{32,48},{64,80},{96,112},{128,144},{160,176},{192,208},{224,240}..., dimensions={0}, use_global_device_ids=true | all-gather | bytes 786432 | tf_op jit(solution)/shard_map/all_gather | solution.py:178
  153.1 1.5 shard_map.85
  154.6 14.8 %all_to_all.51 = f32[16,17,1,128]{3,2,1,0:T(1,128)S(1)} all-to-all(f32[16,17,1,128]{3,2,1,0:T(1,128)S(1)} %bitcast.30), channel_id=1, replica_groups=mesh['samp'=32,'kmer'=16] {'kmer'}, dimensions={0} | all-to-all | bytes 278528 | tf_op jit(solution)/shard_map/all_to_all | solution.py:170
  169.4 0.7 shard_map.86
  (12 shorter events, 0.2 us)
Async XLA Ops:
  0.6 0.8 copy-start.1
  1.4 42.5 %copy-start = (bf16[1,1,32,128,128]{4,3,2,1,0:T(8,128)(2,1)S(1)}, bf16[1,1,32,128,128]{4,3,2,1,0:T(8,128)(2,1)}, u32[]{:S(2)}) copy-start(bf16[1,1,32,128,128]{4,3,2,1,0:T(8,128)(2,1)} %param.9) | copy-start | bytes 3145732
  2.1 15.3 %all-to-all-start.1 = ((bf16[16,64,128]{2,1,0:T(8,128)(2,1)}), bf16[16,64,128]{2,1,0:T(8,128)(2,1)S(1)}, u32[]{:S(2)}, u32[]{:S(2)}) async-start(bf16[16,64,128]{2,1,0:T(8,128)(2,1)} %shard_map.78), calls=%async_computation.1 | async-start | bytes 524288 | tf_op jit(solution)/shard_map/all_to_all | solution.py:174
  10.4 0.7 copy-start.3
  11.1 0.7 copy-start.4
  11.7 0.7 copy-start.5
  17.4 26.5 %all-to-all-start = ((bf16[16,16,128]{2,1,0:T(8,128)(2,1)}), bf16[16,16,128]{2,1,0:T(8,128)(2,1)S(1)}, u32[]{:S(2)}, u32[]{:S(2)}) async-start(bf16[16,16,128]{2,1,0:T(8,128)(2,1)} %get-tuple-element.14), calls=%async_computation | async-start | bytes 131072 | tf_op jit(solution)/shard_map/all_to_all | solution.py:170
  45.3 21.2 %copy-start.2 = (f32[64,128]{1,0:T(8,128)S(1)}, f32[64,128]{1,0:T(8,128)}, u32[]{:S(2)}) copy-start(f32[64,128]{1,0:T(8,128)} %h_ref.3) | copy-start | bytes 98308
  45.3 7.1 %collective-permute-start = (f32[16,72,128]{2,1,0:T(8,128)S(1)}, f32[16,72,128]{2,1,0:T(8,128)S(1)}, u32[]{:S(2)}, u32[]{:S(2)}) collective-permute-start(f32[16,72,128]{2,1,0:T(8,128)S(1)} %slice_bitcast_fusion.2), channel_id=1, source_target_pairs={{0,16},{16,0},{32,48},{48,32},{64,80},{80,64},{96,112},{112,96},{1... | collective-permute-start | bytes 1769480 | tf_op jit(solution)/shard_map/ppermute | solution.py:217
  117.7 5.7 %collective-permute-start.1 = (f32[16,72,128]{2,1,0:T(8,128)S(1)}, f32[16,72,128]{2,1,0:T(8,128)S(1)}, u32[]{:S(2)}, u32[]{:S(2)}) collective-permute-start(f32[16,72,128]{2,1,0:T(8,128)S(1)} %slice_bitcast_fusion), channel_id=1, source_target_pairs={{0,16},{16,0},{32,48},{48,32},{64,80},{80,64},{96,112},{112,96},{1... | collective-permute-start | bytes 1769480 | tf_op jit(solution)/shard_map/ppermute | solution.py:217

commit v6 on v5

--- a/solution.py
+++ b/solution.py
@@ -14,7 +14,8 @@
 N_KMER = 16
 N_CHIP = 16
 OWN = 16
-SUMS = 8
+WIDE = RANK + 1
+AHEAD = (6, 12)
 ROWS = OWN + 1
 
 CORES = [[2 * a, 2 * a + 1] for a in range(N_CHIP)]
@@ -75,36 +76,55 @@
     return copy
 
 
-def ratio_of(g, place, live_ref, values_ref, tiles_ref, h_ref):
-    r, c = place[0, 0, g] & (ROW_TILES - 1), place[0, 0, g] >> 2
-    h_tile = h_ref[c & 1, c >> 1]
-    estimate = jnp.dot(tiles_ref[r], h_tile, preferred_element_type=f32)
+def place_of(place, g):
+    return place[0, 0, g] & (ROW_TILES - 1), place[0, 0, g] >> 2
+
+
+def estimate_of(r, c, tiles_ref, h_ref):
+    return jnp.dot(tiles_ref[r], h_ref[c & 1, c >> 1], preferred_element_type=f32)
+
+
+def ratio_of(g, estimate, live_ref, values_ref):
     ratio = values_ref[g].astype(f32) / estimate
-    ratio = jnp.where(live_ref[g : g + 1, :] > 0.0, ratio, 0.0).astype(bf16)
-    return r, c, h_tile, ratio
-
-
-def numer_h_kernel(place_ref, live_ref, values_ref, w_ref, h_ref, out_ref, place, sem, tiles_ref, flip_ref):
+    return jnp.where(live_ref[g : g + 1, :] > 0.0, ratio, 0.0).astype(bf16)
+
+
+def numer_h_kernel(place_ref, live_ref, values_ref, w_ref, h_ref, out_ref, place, sem, tiles_ref, flip_ref, acc_ref):
     copy = fetch(place_ref, place, sem)
     own_core = lax.axis_index("samp") & 1
     unpack(w_ref, tiles_ref)
     for r in range(ROW_TILES):
         flip_ref[r] = tiles_ref[r].T
     sums = jnp.sum(w_ref[...].astype(f32).reshape(N_KMER * OWN, 2 * RANK), axis=0, keepdims=True)
-    out_ref[:, :, :RANK, :] = jnp.zeros((2, N_CHIP, RANK, TILE), f32)
-    out_ref[:, :, RANK:, :] = jnp.broadcast_to(sums[None, None], (2, N_CHIP, SUMS, TILE))
+    acc_ref[...] = jnp.zeros_like(acc_ref)
     copy.wait()
-    for g in range(CAP):
-        r, c, h_tile, ratio = ratio_of(g, place, live_ref, values_ref, tiles_ref, h_ref)
-        out_ref[jnp.bitwise_xor(c & 1, own_core), c >> 1, :RANK, :] += jnp.dot(flip_ref[r], ratio, preferred_element_type=f32)
+    places = [place_of(place, g) for g in range(CAP)]
+    estimates, ratios = {}, {}
+    for step in range(CAP + sum(AHEAD)):
+        if step < CAP:
+            estimates[step] = estimate_of(*places[step], tiles_ref, h_ref)
+        g = step - AHEAD[0]
+        if 0 <= g < CAP:
+            ratios[g] = ratio_of(g, estimates.pop(g), live_ref, values_ref)
+        g = g - AHEAD[1]
+        if 0 <= g < CAP:
+            r, c = places[g]
+            term = jnp.dot(flip_ref[r], ratios.pop(g), preferred_element_type=f32)
+            acc_ref[jnp.bitwise_xor(c & 1, own_core), c >> 1] += term
+    for half in range(2):
+        for k in range(N_CHIP):
+            out_ref[half, k * WIDE : k * WIDE + RANK, :] = acc_ref[half, k]
+            out_ref[half, k * WIDE + RANK : (k + 1) * WIDE, :] = sums
 
 
 def update_h_kernel(parts_ref, h_ref, own_ref, out_ref):
-    summed = parts_ref[0]
+    summed = parts_ref[:RANK, :]
+    total = parts_ref[RANK:WIDE, :]
     for k in range(1, N_CHIP):
-        summed = summed + parts_ref[k]
-    total = jnp.where(same_rank((RANK, TILE)), summed[RANK : RANK + 1], 0.0)
-    h_new = h_ref[...] * summed[:RANK] / jnp.sum(total, axis=1, keepdims=True)
+        summed = summed + parts_ref[k * WIDE : k * WIDE + RANK, :]
+        total = total + parts_ref[k * WIDE + RANK : (k + 1) * WIDE, :]
+    total = jnp.where(same_rank((RANK, TILE)), total, 0.0)
+    h_new = h_ref[...] * summed / jnp.sum(total, axis=1, keepdims=True)
     own_ref[...] = h_new
     half = h_new.astype(bf16)
     for k in range(N_CHIP):
@@ -122,9 +142,10 @@
     acc_ref[...] = jnp.zeros_like(acc_ref)
     copy.wait()
     for g in range(CAP):
-        r, c, h_tile, ratio = ratio_of(g, place, live_ref, values_ref, tiles_ref, h_ref)
+        r, c = place_of(place, g)
+        ratio = ratio_of(g, estimate_of(r, c, tiles_ref, h_ref), live_ref, values_ref)
         acc_ref[r] += lax.dot_general(
-            ratio, h_tile, (((1,), (1,)), ((), ())), preferred_element_type=f32
+            ratio, h_ref[c & 1, c >> 1], (((1,), (1,)), ((), ())), preferred_element_type=f32
         )
     for k in range(N_KMER):
         r, q = k // 4, k % 4
@@ -186,6 +207,7 @@
     w_own, h_own = shape((OWN, 2 * RANK), f32), shape((RANK, TILE), f32)
     tiles = pltpu.VMEM((ROW_TILES, TILE, RANK), bf16)
     flip = pltpu.VMEM((ROW_TILES, RANK, TILE), bf16)
+    halves = pltpu.VMEM((2, N_CHIP, RANK, TILE), f32)
     acc = pltpu.VMEM((ROW_TILES, TILE, RANK), f32)
     wide = [VMEM] * 5
     fetched = [pltpu.SMEM((1, 1, CAP), jnp.int32), pltpu.SemaphoreType.DMA(())]
@@ -194,7 +216,7 @@
     start_h = call(start_h_kernel, h_spread, [VMEM])
     place = shape((1, 1, CAP), jnp.int32)
     start_w = call(start_w_kernel, (w_own, w_spread, live, place), [SMEM] * 3 + [VMEM])
-    numer_h = call(numer_h_kernel, shape((2, N_CHIP, RANK + SUMS, TILE), f32), wide, fetched + [tiles, flip])
+    numer_h = call(numer_h_kernel, shape((2, N_CHIP * WIDE, TILE), f32), wide, fetched + [tiles, flip, halves])
     update_h = call(update_h_kernel, (h_own, h_spread), [VMEM] * 2)
     numer_w = call(numer_w_kernel, shape((N_KMER * ROWS, TILE), f32), wide, fetched + [tiles, acc])
     update_w = call(update_w_kernel, (w_own, w_spread), [VMEM] * 2)
@@ -215,7 +237,8 @@
     for sweep in range(ITERS):
         numer = numer_h(*slots, values, w_panel, h_panel)
         numer = numer[0] + lax.ppermute(numer[1], "samp", swap(1))
-        h_own, h_out = update_h(to_chips(numer), h_own)
+        parts = to_chips(numer.reshape(N_CHIP, WIDE, 1, TILE)).reshape(N_CHIP * WIDE, TILE)
+        h_own, h_out = update_h(parts, h_own)
         h_panel = panel_of(h_out)
         parts = numer_w(*slots, values, w_panel, h_panel).reshape(N_KMER, ROWS, 1, TILE)
         parts = to_kmer(parts).reshape(N_KMER * ROWS, TILE)

time: 172 us -> 171 us (level)
  no operation moved by 1% of the time
where the time goes in v6:
time: 171 us; the launch traced here: 169 us
  blocking collectives  110 us (64%)
  starting transfers between devices  31.9 us (19%)
  waiting for transfers between devices  14.3 us (8%)
  Pallas kernels  8.54 us (5%)
  local copies, waits for them, and re-layouts  2.86 us (2%)
    all_to_all x4, blocking collectives, to_chips(): return lax.all_to_all(x, 'samp', 0, 0, axis_index_groups=CHIPS)  48.8 us
    all_to_all x3, blocking collectives, to_kmer(): return lax.all_to_all(x, 'kmer', 0, 0)  47.5 us
    all_to_all x1, starting transfers between devices, to_kmer(): return lax.all_to_all(x, 'kmer', 0, 0)  14.8 us
    all_gather x3, blocking collectives, panel_of(): lax.all_gather(to_chips(spread), 'samp', axis=0, axis_index_groups=CORES)  13.2 us
    ppermute x2, starting transfers between devices, body(): numer = numer[0] + lax.ppermute(numer[1], 'samp', swap(1))  9.52 us
    all_to_all x1, starting transfers between devices, to_chips(): return lax.all_to_all(x, 'samp', 0, 0, axis_index_groups=CHIPS)  7.58 us
    all_to_all x1, waiting for transfers between devices, to_kmer(): return lax.all_to_all(x, 'kmer', 0, 0)  7.47 us
    all_to_all x1, waiting for transfers between devices, to_chips(): return lax.all_to_all(x, 'samp', 0, 0, axis_index_groups=CHIPS)  3.73 us
  transfers between devices with their start and end apart: 4, of which 4 were waited for; matrix products, arithmetic and copies ran while one was open for 0% of the time, Pallas kernels for 1%

profile of v6, /device:TPU:1, one launch (start us, length us, event | category | flops | bytes accessed | tf_op | source)
XLA Modules:
  0.0 168.6 jit_solution(9538214080675363396)
XLA Ops:
  0.6 0.7 copy-done.1
  1.4 0.7 shard_map.78
  2.1 7.6 %all-to-all-start.1 = ((bf16[16,64,128]{2,1,0:T(8,128)(2,1)}), bf16[16,64,128]{2,1,0:T(8,128)(2,1)S(1)}, u32[]{:S(2)}, u32[]{:S(2)}) async-start(bf16[16,64,128]{2,1,0:T(8,128)(2,1)} %shard_map.78), calls=%async_computation.1 | async-start | bytes 524288 | tf_op jit(solution)/shard_map/all_to_all | solution.py:195
  10.4 0.7 copy-done.3
  11.1 0.7 copy-done.4
  11.7 0.7 copy-done.5
  12.4 1.3 shard_map.77
  13.7 3.7 %all-to-all-done.1 = bf16[16,64,128]{2,1,0:T(8,128)(2,1)S(1)} async-done(((bf16[16,64,128]{2,1,0:T(8,128)(2,1)}), bf16[16,64,128]{2,1,0:T(8,128)(2,1)S(1)}, u32[]{:S(2)}, u32[]{:S(2)}) %all-to-all-start.1) | async-done | bytes 262176 | tf_op jit(solution)/shard_map/all_to_all | solution.py:195
  17.4 14.8 %all-to-all-start = ((bf16[16,16,128]{2,1,0:T(8,128)(2,1)}), bf16[16,16,128]{2,1,0:T(8,128)(2,1)S(1)}, u32[]{:S(2)}, u32[]{:S(2)}) async-start(bf16[16,16,128]{2,1,0:T(8,128)(2,1)} %get-tuple-element.14), calls=%async_computation | async-start | bytes 131072 | tf_op jit(solution)/shard_map/all_to_all | solution.py:191
  32.2 4.2 %all-gather = bf16[32,64,128]{2,1,0:T(8,128)(2,1)S(1)} all-gather(bf16[16,64,128]{2,1,0:T(8,128)(2,1)S(1)} %all-to-all-done.1), channel_id=2, replica_groups={{0,16},{32,48},{64,80},{96,112},{128,144},{160,176},{192,208},{224,240}..., dimensions={0}, use_global_device_ids=true | all-gather | bytes 786432 | tf_op jit(solution)/shard_map/all_gather | solution.py:199
  36.4 7.5 %all-to-all-done.w_ref = bf16[16,16,128]{2,1,0:T(8,128)(2,1)S(1)} async-done(((bf16[16,16,128]{2,1,0:T(8,128)(2,1)}), bf16[16,16,128]{2,1,0:T(8,128)(2,1)S(1)}, u32[]{:S(2)}, u32[]{:S(2)}) %all-to-all-start) | async-done | bytes 65568 | tf_op jit(solution)/shard_map/all_to_all | solution.py:191
  43.8 1.3 shard_map.79
  45.2 5.4 %collective-permute-start = (f32[1040,128]{1,0:T(8,128)S(1)}, f32[1040,128]{1,0:T(8,128)S(1)}, u32[]{:S(2)}, u32[]{:S(2)}) collective-permute-start(f32[1040,128]{1,0:T(8,128)S(1)} %slice_bitcast_fusion.2), channel_id=1, source_target_pairs={{0,16},{16,0},{32,48},{48,32},{64,80},{80,64},{96,112},{112,96},{1... | collective-permute-start | bytes 1597448 | tf_op jit(solution)/shard_map/ppermute | solution.py:239
  50.6 1.5 collective-permute-done
  52.2 13.6 %all_to_all.45 = f32[16,65,1,128]{3,2,1,0:T(1,128)S(1)} all-to-all(f32[16,65,1,128]{3,2,1,0:T(1,128)S(1)} %bitcast.38), channel_id=1, replica_groups={{0,32,64,96,128,160,192,224,256,288,320,352,384,416,448,480},{16,48,80,..., dimensions={0} | all-to-all | bytes 1064960 | tf_op jit(solution)/shard_map/all_to_all | solution.py:195
  65.9 0.1 shard_map.80
  66.0 10.8 %all_to_all.46 = bf16[16,64,128]{2,1,0:T(8,128)(2,1)S(1)} all-to-all(bf16[16,64,128]{2,1,0:T(8,128)(2,1)S(1)} %get-tuple-element.15), channel_id=1, replica_groups={{0,32,64,96,128,160,192,224,256,288,320,352,384,416,448,480},{16,48,80,..., dimensions={0} | all-to-all | bytes 524288 | tf_op jit(solution)/shard_map/all_to_all | solution.py:195
  76.7 4.5 %all-gather.1 = bf16[32,64,128]{2,1,0:T(8,128)(2,1)S(1)} all-gather(bf16[16,64,128]{2,1,0:T(8,128)(2,1)S(1)} %all_to_all.46), channel_id=3, replica_groups={{0,16},{32,48},{64,80},{96,112},{128,144},{160,176},{192,208},{224,240}..., dimensions={0}, use_global_device_ids=true | all-gather | bytes 786432 | tf_op jit(solution)/shard_map/all_gather | solution.py:199
  81.3 1.5 shard_map.81
  82.8 14.7 %all_to_all.47 = f32[16,17,1,128]{3,2,1,0:T(1,128)S(1)} all-to-all(f32[16,17,1,128]{3,2,1,0:T(1,128)S(1)} %bitcast.37), channel_id=1, replica_groups=mesh['samp'=32,'kmer'=16] {'kmer'}, dimensions={0} | all-to-all | bytes 278528 | tf_op jit(solution)/shard_map/all_to_all | solution.py:191
  97.5 18.1 %all_to_all.48.w_ref = bf16[16,16,128]{2,1,0:T(8,128)(2,1)S(1)} all-to-all(bf16[16,16,128]{2,1,0:T(8,128)(2,1)S(1)} %get-tuple-element.17), channel_id=1, replica_groups=mesh['samp'=32,'kmer'=16] {'kmer'}, dimensions={0} | all-to-all | bytes 131072 | tf_op jit(solution)/shard_map/all_to_all | solution.py:191
  115.6 1.3 shard_map.83
  116.9 4.1 %collective-permute-start.1 = (f32[1040,128]{1,0:T(8,128)S(1)}, f32[1040,128]{1,0:T(8,128)S(1)}, u32[]{:S(2)}, u32[]{:S(2)}) collective-permute-start(f32[1040,128]{1,0:T(8,128)S(1)} %slice_bitcast_fusion), channel_id=1, source_target_pairs={{0,16},{16,0},{32,48},{48,32},{64,80},{80,64},{96,112},{112,96},{1... | collective-permute-start | bytes 1597448 | tf_op jit(solution)/shard_map/ppermute | solution.py:239
  121.0 1.5 collective-permute-done.1
  122.5 0.1 fusion
  122.6 13.6 %all_to_all.49 = f32[16,65,1,128]{3,2,1,0:T(1,128)S(1)} all-to-all(f32[16,65,1,128]{3,2,1,0:T(1,128)S(1)} %bitcast.39), channel_id=1, replica_groups={{0,32,64,96,128,160,192,224,256,288,320,352,384,416,448,480},{16,48,80,..., dimensions={0} | all-to-all | bytes 1064960 | tf_op jit(solution)/shard_map/all_to_all | solution.py:195
  136.2 0.1 shard_map.84
  136.4 10.7 %all_to_all.50 = bf16[16,64,128]{2,1,0:T(8,128)(2,1)S(1)} all-to-all(bf16[16,64,128]{2,1,0:T(8,128)(2,1)S(1)} %get-tuple-element.19), channel_id=1, replica_groups={{0,32,64,96,128,160,192,224,256,288,320,352,384,416,448,480},{16,48,80,..., dimensions={0} | all-to-all | bytes 524288 | tf_op jit(solution)/shard_map/all_to_all | solution.py:195
  147.1 4.5 %all-gather.2 = bf16[32,64,128]{2,1,0:T(8,128)(2,1)S(1)} all-gather(bf16[16,64,128]{2,1,0:T(8,128)(2,1)S(1)} %all_to_all.50), channel_id=4, replica_groups={{0,16},{32,48},{64,80},{96,112},{128,144},{160,176},{192,208},{224,240}..., dimensions={0}, use_global_device_ids=true | all-gather | bytes 786432 | tf_op jit(solution)/shard_map/all_gather | solution.py:199
  151.6 1.5 shard_map.85
  153.1 14.8 %all_to_all.51 = f32[16,17,1,128]{3,2,1,0:T(1,128)S(1)} all-to-all(f32[16,17,1,128]{3,2,1,0:T(1,128)S(1)} %bitcast.36), channel_id=1, replica_groups=mesh['samp'=32,'kmer'=16] {'kmer'}, dimensions={0} | all-to-all | bytes 278528 | tf_op jit(solution)/shard_map/all_to_all | solution.py:191
  167.9 0.7 shard_map.86
  (12 shorter events, 0.2 us)
Async XLA Ops:
  0.6 0.8 copy-start.1
  1.4 42.5 %copy-start = (bf16[1,1,32,128,128]{4,3,2,1,0:T(8,128)(2,1)S(1)}, bf16[1,1,32,128,128]{4,3,2,1,0:T(8,128)(2,1)}, u32[]{:S(2)}) copy-start(bf16[1,1,32,128,128]{4,3,2,1,0:T(8,128)(2,1)} %param.9) | copy-start | bytes 3145732
  2.1 15.3 %all-to-all-start.1 = ((bf16[16,64,128]{2,1,0:T(8,128)(2,1)}), bf16[16,64,128]{2,1,0:T(8,128)(2,1)S(1)}, u32[]{:S(2)}, u32[]{:S(2)}) async-start(bf16[16,64,128]{2,1,0:T(8,128)(2,1)} %shard_map.78), calls=%async_computation.1 | async-start | bytes 524288 | tf_op jit(solution)/shard_map/all_to_all | solution.py:195
  10.4 0.7 copy-start.3
  11.1 0.7 copy-start.4
  11.7 0.7 copy-start.5
  17.4 26.5 %all-to-all-start = ((bf16[16,16,128]{2,1,0:T(8,128)(2,1)}), bf16[16,16,128]{2,1,0:T(8,128)(2,1)S(1)}, u32[]{:S(2)}, u32[]{:S(2)}) async-start(bf16[16,16,128]{2,1,0:T(8,128)(2,1)} %get-tuple-element.14), calls=%async_computation | async-start | bytes 131072 | tf_op jit(solution)/shard_map/all_to_all | solution.py:191
  45.2 20.7 %copy-start.2 = (f32[64,128]{1,0:T(8,128)S(1)}, f32[64,128]{1,0:T(8,128)}, u32[]{:S(2)}) copy-start(f32[64,128]{1,0:T(8,128)} %h_ref.3) | copy-start | bytes 98308
  45.2 7.0 %collective-permute-start = (f32[1040,128]{1,0:T(8,128)S(1)}, f32[1040,128]{1,0:T(8,128)S(1)}, u32[]{:S(2)}, u32[]{:S(2)}) collective-permute-start(f32[1040,128]{1,0:T(8,128)S(1)} %slice_bitcast_fusion.2), channel_id=1, source_target_pairs={{0,16},{16,0},{32,48},{48,32},{64,80},{80,64},{96,112},{112,96},{1... | collective-permute-start | bytes 1597448 | tf_op jit(solution)/shard_map/ppermute | solution.py:239
  116.9 5.6 %collective-permute-start.1 = (f32[1040,128]{1,0:T(8,128)S(1)}, f32[1040,128]{1,0:T(8,128)S(1)}, u32[]{:S(2)}, u32[]{:S(2)}) collective-permute-start(f32[1040,128]{1,0:T(8,128)S(1)} %slice_bitcast_fusion), channel_id=1, source_target_pairs={{0,16},{16,0},{32,48},{48,32},{64,80},{80,64},{96,112},{112,96},{1... | collective-permute-start | bytes 1597448 | tf_op jit(solution)/shard_map/ppermute | solution.py:239

commit v7 on v6

--- a/solution.py
+++ b/solution.py
@@ -24,7 +24,6 @@
 f32 = jnp.float32
 bf16 = jnp.bfloat16
 VMEM = pl.BlockSpec(memory_space=pltpu.VMEM)
-SMEM = pl.BlockSpec(memory_space=pltpu.SMEM)
 
 
 def call(kernel, out_shape, in_specs, scratch=(), out_spec=VMEM):
@@ -32,7 +31,7 @@
         kernel,
         out_shape=out_shape,
         in_specs=in_specs,
-        out_specs=jax.tree.map(lambda x: SMEM if x.dtype == jnp.int32 else out_spec, out_shape),
+        out_specs=jax.tree.map(lambda _: out_spec, out_shape),
         scratch_shapes=scratch,
         compiler_params=pltpu.CompilerParams(vmem_limit_bytes=32 * 2**20),
     )
@@ -50,11 +49,10 @@
         h_out[k] = h_half
 
 
-def start_w_kernel(rows, cols, count, w_ref, own_ref, w_out, live_ref, place):
-    for g in range(CAP):
-        place[0, 0, g] = cols[0, 0, g] * ROW_TILES + rows[0, 0, g]
+def start_w_kernel(rows, cols, count, w_ref, own_ref, w_out, live_ref, place_ref):
+    place_ref[...] = cols[...] * ROW_TILES + rows[...]
     slot = lax.broadcasted_iota(jnp.int32, (CAP, TILE), 0)
-    live_ref[...] = (slot < count[0, 0]).astype(f32)
+    live_ref[...] = (slot < count[...]).astype(f32)
     own_ref[:, :RANK] = w_ref[:OWN, :]
     own_ref[:, RANK:] = w_ref[OWN:, :]
     half = own_ref[...].astype(bf16)
@@ -70,14 +68,9 @@
         tiles_ref[r, 32 * q + OWN : 32 * q + 2 * OWN, :] = block[:, RANK:]
 
 
-def fetch(place_ref, place, sem):
-    copy = pltpu.make_async_copy(place_ref, place, sem)
-    copy.start()
-    return copy
-
-
-def place_of(place, g):
-    return place[0, 0, g] & (ROW_TILES - 1), place[0, 0, g] >> 2
+def places_of(place_ref):
+    place = place_ref[0]
+    return [(place[0, g] & (ROW_TILES - 1), place[0, g] >> 2) for g in range(CAP)]
 
 
 def estimate_of(r, c, tiles_ref, h_ref):
@@ -89,16 +82,14 @@
     return jnp.where(live_ref[g : g + 1, :] > 0.0, ratio, 0.0).astype(bf16)
 
 
-def numer_h_kernel(place_ref, live_ref, values_ref, w_ref, h_ref, out_ref, place, sem, tiles_ref, flip_ref, acc_ref):
-    copy = fetch(place_ref, place, sem)
+def numer_h_kernel(place_ref, live_ref, values_ref, w_ref, h_ref, out_ref, tiles_ref, flip_ref, acc_ref):
     own_core = lax.axis_index("samp") & 1
     unpack(w_ref, tiles_ref)
     for r in range(ROW_TILES):
         flip_ref[r] = tiles_ref[r].T
     sums = jnp.sum(w_ref[...].astype(f32).reshape(N_KMER * OWN, 2 * RANK), axis=0, keepdims=True)
     acc_ref[...] = jnp.zeros_like(acc_ref)
-    copy.wait()
-    places = [place_of(place, g) for g in range(CAP)]
+    places = places_of(place_ref)
     estimates, ratios = {}, {}
     for step in range(CAP + sum(AHEAD)):
         if step < CAP:
@@ -131,8 +122,7 @@
         out_ref[k] = half
 
 
-def numer_w_kernel(place_ref, live_ref, values_ref, w_ref, h_ref, out_ref, place, sem, tiles_ref, acc_ref):
-    copy = fetch(place_ref, place, sem)
+def numer_w_kernel(place_ref, live_ref, values_ref, w_ref, h_ref, out_ref, tiles_ref, acc_ref):
     unpack(w_ref, tiles_ref)
     sums = jnp.zeros((RANK, TILE), f32)
     for c in range(COL_TILES):
@@ -140,9 +130,7 @@
     sums = jnp.where(same_rank((RANK, TILE)), jnp.sum(sums, axis=1, keepdims=True), 0.0)
     sums = jnp.sum(sums, axis=0, keepdims=True)
     acc_ref[...] = jnp.zeros_like(acc_ref)
-    copy.wait()
-    for g in range(CAP):
-        r, c = place_of(place, g)
+    for g, (r, c) in enumerate(places_of(place_ref)):
         ratio = ratio_of(g, estimate_of(r, c, tiles_ref, h_ref), live_ref, values_ref)
         acc_ref[r] += lax.dot_general(
             ratio, h_ref[c & 1, c >> 1], (((1,), (1,)), ((), ())), preferred_element_type=f32
@@ -210,15 +198,14 @@
     halves = pltpu.VMEM((2, N_CHIP, RANK, TILE), f32)
     acc = pltpu.VMEM((ROW_TILES, TILE, RANK), f32)
     wide = [VMEM] * 5
-    fetched = [pltpu.SMEM((1, 1, CAP), jnp.int32), pltpu.SemaphoreType.DMA(())]
 
     live = shape((CAP, TILE), f32)
     start_h = call(start_h_kernel, h_spread, [VMEM])
     place = shape((1, 1, CAP), jnp.int32)
-    start_w = call(start_w_kernel, (w_own, w_spread, live, place), [SMEM] * 3 + [VMEM])
-    numer_h = call(numer_h_kernel, shape((2, N_CHIP * WIDE, TILE), f32), wide, fetched + [tiles, flip, halves])
+    start_w = call(start_w_kernel, (w_own, w_spread, live, place), [VMEM] * 4)
+    numer_h = call(numer_h_kernel, shape((2, N_CHIP * WIDE, TILE), f32), wide, [tiles, flip, halves])
     update_h = call(update_h_kernel, (h_own, h_spread), [VMEM] * 2)
-    numer_w = call(numer_w_kernel, shape((N_KMER * ROWS, TILE), f32), wide, fetched + [tiles, acc])
+    numer_w = call(numer_w_kernel, shape((N_KMER * ROWS, TILE), f32), wide, [tiles, acc])
     update_w = call(update_w_kernel, (w_own, w_spread), [VMEM] * 2)
     last_w = call(
         last_w_kernel,

time: 171 us -> 169 us (0.988)
  Pallas kernels: 8.54 us -> 6.24 us
  transfers between devices with their start and end apart: 4 -> 4, of which waited for: 4 -> 4; matrix products, arithmetic and copies ran while one was open for 0% -> 0% of each run, Pallas kernels for 1% -> 0%
where the time goes in v7:
time: 169 us; the launch traced here: 167 us
  blocking collectives  110 us (65%)
  starting transfers between devices  31.9 us (19%)
  waiting for transfers between devices  14.8 us (9%)
  Pallas kernels  6.24 us (4%)
  local copies, waits for them, and re-layouts  2.86 us (2%)
    all_to_all x4, blocking collectives, to_chips(): return lax.all_to_all(x, 'samp', 0, 0, axis_index_groups=CHIPS)  48.8 us
    all_to_all x3, blocking collectives, to_kmer(): return lax.all_to_all(x, 'kmer', 0, 0)  47.5 us
    all_to_all x1, starting transfers between devices, to_kmer(): return lax.all_to_all(x, 'kmer', 0, 0)  14.8 us
    all_gather x3, blocking collectives, panel_of(): lax.all_gather(to_chips(spread), 'samp', axis=0, axis_index_groups=CORES)  13.2 us
    ppermute x2, starting transfers between devices, body(): numer = numer[0] + lax.ppermute(numer[1], 'samp', swap(1))  9.53 us
    all_to_all x1, starting transfers between devices, to_chips(): return lax.all_to_all(x, 'samp', 0, 0, axis_index_groups=CHIPS)  7.58 us
    all_to_all x1, waiting for transfers between devices, to_kmer(): return lax.all_to_all(x, 'kmer', 0, 0)  7.47 us
    all_to_all x1, waiting for transfers between devices, to_chips(): return lax.all_to_all(x, 'samp', 0, 0, axis_index_groups=CHIPS)  4.29 us
  transfers between devices with their start and end apart: 4, of which 4 were waited for; matrix products, arithmetic and copies ran while one was open for 0% of the time, Pallas kernels for 0%

profile of v7, /device:TPU:1, one launch (start us, length us, event | category | flops | bytes accessed | tf_op | source)
XLA Modules:
  0.0 166.9 jit_solution(1737344217401118197)
XLA Ops:
  0.6 0.7 copy-done.1
  1.4 0.7 shard_map.78
  2.1 7.6 %all-to-all-start.1 = ((bf16[16,64,128]{2,1,0:T(8,128)(2,1)}), bf16[16,64,128]{2,1,0:T(8,128)(2,1)S(1)}, u32[]{:S(2)}, u32[]{:S(2)}) async-start(bf16[16,64,128]{2,1,0:T(8,128)(2,1)} %shard_map.78), calls=%async_computation.1 | async-start | bytes 524288 | tf_op jit(solution)/shard_map/all_to_all | solution.py:183
  10.4 0.7 copy-done.3
  11.1 0.7 copy-done.4
  11.7 0.7 copy-done.5
  12.4 0.7 shard_map.77
  13.1 4.3 %all-to-all-done.1 = bf16[16,64,128]{2,1,0:T(8,128)(2,1)S(1)} async-done(((bf16[16,64,128]{2,1,0:T(8,128)(2,1)}), bf16[16,64,128]{2,1,0:T(8,128)(2,1)S(1)}, u32[]{:S(2)}, u32[]{:S(2)}) %all-to-all-start.1) | async-done | bytes 262176 | tf_op jit(solution)/shard_map/all_to_all | solution.py:183
  17.4 14.8 %all-to-all-start = ((bf16[16,16,128]{2,1,0:T(8,128)(2,1)}), bf16[16,16,128]{2,1,0:T(8,128)(2,1)S(1)}, u32[]{:S(2)}, u32[]{:S(2)}) async-start(bf16[16,16,128]{2,1,0:T(8,128)(2,1)} %get-tuple-element.14), calls=%async_computation | async-start | bytes 131072 | tf_op jit(solution)/shard_map/all_to_all | solution.py:179
  32.2 4.2 %all-gather = bf16[32,64,128]{2,1,0:T(8,128)(2,1)S(1)} all-gather(bf16[16,64,128]{2,1,0:T(8,128)(2,1)S(1)} %all-to-all-done.1), channel_id=2, replica_groups={{0,16},{32,48},{64,80},{96,112},{128,144},{160,176},{192,208},{224,240}..., dimensions={0}, use_global_device_ids=true | all-gather | bytes 786432 | tf_op jit(solution)/shard_map/all_gather | solution.py:187
  36.4 7.5 %all-to-all-done.w_ref = bf16[16,16,128]{2,1,0:T(8,128)(2,1)S(1)} async-done(((bf16[16,16,128]{2,1,0:T(8,128)(2,1)}), bf16[16,16,128]{2,1,0:T(8,128)(2,1)S(1)}, u32[]{:S(2)}, u32[]{:S(2)}) %all-to-all-start) | async-done | bytes 65568 | tf_op jit(solution)/shard_map/all_to_all | solution.py:179
  43.8 0.9 shard_map.79
  44.8 5.5 %collective-permute-start = (f32[1040,128]{1,0:T(8,128)S(1)}, f32[1040,128]{1,0:T(8,128)S(1)}, u32[]{:S(2)}, u32[]{:S(2)}) collective-permute-start(f32[1040,128]{1,0:T(8,128)S(1)} %slice_bitcast_fusion.2), channel_id=1, source_target_pairs={{0,16},{16,0},{32,48},{48,32},{64,80},{80,64},{96,112},{112,96},{1... | collective-permute-start | bytes 1597448 | tf_op jit(solution)/shard_map/ppermute | solution.py:226
  50.3 1.5 collective-permute-done
  51.8 13.6 %all_to_all.45 = f32[16,65,1,128]{3,2,1,0:T(1,128)S(1)} all-to-all(f32[16,65,1,128]{3,2,1,0:T(1,128)S(1)} %bitcast.38), channel_id=1, replica_groups={{0,32,64,96,128,160,192,224,256,288,320,352,384,416,448,480},{16,48,80,..., dimensions={0} | all-to-all | bytes 1064960 | tf_op jit(solution)/shard_map/all_to_all | solution.py:183
  65.5 0.1 shard_map.80
  65.6 10.8 %all_to_all.46 = bf16[16,64,128]{2,1,0:T(8,128)(2,1)S(1)} all-to-all(bf16[16,64,128]{2,1,0:T(8,128)(2,1)S(1)} %get-tuple-element.15), channel_id=1, replica_groups={{0,32,64,96,128,160,192,224,256,288,320,352,384,416,448,480},{16,48,80,..., dimensions={0} | all-to-all | bytes 524288 | tf_op jit(solution)/shard_map/all_to_all | solution.py:183
  76.4 4.5 %all-gather.1 = bf16[32,64,128]{2,1,0:T(8,128)(2,1)S(1)} all-gather(bf16[16,64,128]{2,1,0:T(8,128)(2,1)S(1)} %all_to_all.46), channel_id=3, replica_groups={{0,16},{32,48},{64,80},{96,112},{128,144},{160,176},{192,208},{224,240}..., dimensions={0}, use_global_device_ids=true | all-gather | bytes 786432 | tf_op jit(solution)/shard_map/all_gather | solution.py:187
  80.9 1.0 shard_map.81
  81.9 14.7 %all_to_all.47 = f32[16,17,1,128]{3,2,1,0:T(1,128)S(1)} all-to-all(f32[16,17,1,128]{3,2,1,0:T(1,128)S(1)} %bitcast.37), channel_id=1, replica_groups=mesh['samp'=32,'kmer'=16] {'kmer'}, dimensions={0} | all-to-all | bytes 278528 | tf_op jit(solution)/shard_map/all_to_all | solution.py:179
  96.6 18.1 %all_to_all.48.w_ref = bf16[16,16,128]{2,1,0:T(8,128)(2,1)S(1)} all-to-all(bf16[16,16,128]{2,1,0:T(8,128)(2,1)S(1)} %get-tuple-element.17), channel_id=1, replica_groups=mesh['samp'=32,'kmer'=16] {'kmer'}, dimensions={0} | all-to-all | bytes 131072 | tf_op jit(solution)/shard_map/all_to_all | solution.py:179
  114.7 0.9 shard_map.83
  115.6 4.1 %collective-permute-start.1 = (f32[1040,128]{1,0:T(8,128)S(1)}, f32[1040,128]{1,0:T(8,128)S(1)}, u32[]{:S(2)}, u32[]{:S(2)}) collective-permute-start(f32[1040,128]{1,0:T(8,128)S(1)} %slice_bitcast_fusion), channel_id=1, source_target_pairs={{0,16},{16,0},{32,48},{48,32},{64,80},{80,64},{96,112},{112,96},{1... | collective-permute-start | bytes 1597448 | tf_op jit(solution)/shard_map/ppermute | solution.py:226
  119.7 1.5 collective-permute-done.1
  121.2 0.1 fusion
  121.3 13.6 %all_to_all.49 = f32[16,65,1,128]{3,2,1,0:T(1,128)S(1)} all-to-all(f32[16,65,1,128]{3,2,1,0:T(1,128)S(1)} %bitcast.39), channel_id=1, replica_groups={{0,32,64,96,128,160,192,224,256,288,320,352,384,416,448,480},{16,48,80,..., dimensions={0} | all-to-all | bytes 1064960 | tf_op jit(solution)/shard_map/all_to_all | solution.py:183
  135.0 0.1 shard_map.84
  135.1 10.8 %all_to_all.50 = bf16[16,64,128]{2,1,0:T(8,128)(2,1)S(1)} all-to-all(bf16[16,64,128]{2,1,0:T(8,128)(2,1)S(1)} %get-tuple-element.19), channel_id=1, replica_groups={{0,32,64,96,128,160,192,224,256,288,320,352,384,416,448,480},{16,48,80,..., dimensions={0} | all-to-all | bytes 524288 | tf_op jit(solution)/shard_map/all_to_all | solution.py:183
  145.8 4.5 %all-gather.2 = bf16[32,64,128]{2,1,0:T(8,128)(2,1)S(1)} all-gather(bf16[16,64,128]{2,1,0:T(8,128)(2,1)S(1)} %all_to_all.50), channel_id=4, replica_groups={{0,16},{32,48},{64,80},{96,112},{128,144},{160,176},{192,208},{224,240}..., dimensions={0}, use_global_device_ids=true | all-gather | bytes 786432 | tf_op jit(solution)/shard_map/all_gather | solution.py:187
  150.4 1.0 shard_map.85
  151.4 14.8 %all_to_all.51 = f32[16,17,1,128]{3,2,1,0:T(1,128)S(1)} all-to-all(f32[16,17,1,128]{3,2,1,0:T(1,128)S(1)} %bitcast.36), channel_id=1, replica_groups=mesh['samp'=32,'kmer'=16] {'kmer'}, dimensions={0} | all-to-all | bytes 278528 | tf_op jit(solution)/shard_map/all_to_all | solution.py:179
  166.2 0.7 shard_map.86
  (12 shorter events, 0.2 us)
Async XLA Ops:
  0.6 0.8 copy-start.1
  1.4 42.5 %copy-start = (bf16[1,1,32,128,128]{4,3,2,1,0:T(8,128)(2,1)S(1)}, bf16[1,1,32,128,128]{4,3,2,1,0:T(8,128)(2,1)}, u32[]{:S(2)}) copy-start(bf16[1,1,32,128,128]{4,3,2,1,0:T(8,128)(2,1)} %param.9) | copy-start | bytes 3145732
  2.1 15.3 %all-to-all-start.1 = ((bf16[16,64,128]{2,1,0:T(8,128)(2,1)}), bf16[16,64,128]{2,1,0:T(8,128)(2,1)S(1)}, u32[]{:S(2)}, u32[]{:S(2)}) async-start(bf16[16,64,128]{2,1,0:T(8,128)(2,1)} %shard_map.78), calls=%async_computation.1 | async-start | bytes 524288 | tf_op jit(solution)/shard_map/all_to_all | solution.py:183
  10.4 0.7 copy-start.3
  11.1 0.7 copy-start.4
  11.7 0.7 copy-start.5
  17.4 26.5 %all-to-all-start = ((bf16[16,16,128]{2,1,0:T(8,128)(2,1)}), bf16[16,16,128]{2,1,0:T(8,128)(2,1)S(1)}, u32[]{:S(2)}, u32[]{:S(2)}) async-start(bf16[16,16,128]{2,1,0:T(8,128)(2,1)} %get-tuple-element.14), calls=%async_computation | async-start | bytes 131072 | tf_op jit(solution)/shard_map/all_to_all | solution.py:179
  44.8 20.7 %copy-start.2 = (f32[64,128]{1,0:T(8,128)S(1)}, f32[64,128]{1,0:T(8,128)}, u32[]{:S(2)}) copy-start(f32[64,128]{1,0:T(8,128)} %h_ref.3) | copy-start | bytes 98308
  44.8 7.0 %collective-permute-start = (f32[1040,128]{1,0:T(8,128)S(1)}, f32[1040,128]{1,0:T(8,128)S(1)}, u32[]{:S(2)}, u32[]{:S(2)}) collective-permute-start(f32[1040,128]{1,0:T(8,128)S(1)} %slice_bitcast_fusion.2), channel_id=1, source_target_pairs={{0,16},{16,0},{32,48},{48,32},{64,80},{80,64},{96,112},{112,96},{1... | collective-permute-start | bytes 1597448 | tf_op jit(solution)/shard_map/ppermute | solution.py:226
  115.6 5.6 %collective-permute-start.1 = (f32[1040,128]{1,0:T(8,128)S(1)}, f32[1040,128]{1,0:T(8,128)S(1)}, u32[]{:S(2)}, u32[]{:S(2)}) collective-permute-start(f32[1040,128]{1,0:T(8,128)S(1)} %slice_bitcast_fusion), channel_id=1, source_target_pairs={{0,16},{16,0},{32,48},{48,32},{64,80},{80,64},{96,112},{112,96},{1... | collective-permute-start | bytes 1597448 | tf_op jit(solution)/shard_map/ppermute | solution.py:226

commit v8 on v7

--- a/solution.py
+++ b/solution.py
@@ -82,7 +82,7 @@
     return jnp.where(live_ref[g : g + 1, :] > 0.0, ratio, 0.0).astype(bf16)
 
 
-def numer_h_kernel(place_ref, live_ref, values_ref, w_ref, h_ref, out_ref, tiles_ref, flip_ref, acc_ref):
+def numer_h_kernel(place_ref, live_ref, values_ref, w_ref, h_ref, own_ref, other_ref, tiles_ref, flip_ref, acc_ref):
     own_core = lax.axis_index("samp") & 1
     unpack(w_ref, tiles_ref)
     for r in range(ROW_TILES):
@@ -102,10 +102,10 @@
             r, c = places[g]
             term = jnp.dot(flip_ref[r], ratios.pop(g), preferred_element_type=f32)
             acc_ref[jnp.bitwise_xor(c & 1, own_core), c >> 1] += term
-    for half in range(2):
+    for half, out_ref in enumerate((own_ref, other_ref)):
         for k in range(N_CHIP):
-            out_ref[half, k * WIDE : k * WIDE + RANK, :] = acc_ref[half, k]
-            out_ref[half, k * WIDE + RANK : (k + 1) * WIDE, :] = sums
+            out_ref[k * WIDE : k * WIDE + RANK, :] = acc_ref[half, k]
+            out_ref[k * WIDE + RANK : (k + 1) * WIDE, :] = sums
 
 
 def update_h_kernel(parts_ref, h_ref, own_ref, out_ref):
@@ -203,7 +203,7 @@
     start_h = call(start_h_kernel, h_spread, [VMEM])
     place = shape((1, 1, CAP), jnp.int32)
     start_w = call(start_w_kernel, (w_own, w_spread, live, place), [VMEM] * 4)
-    numer_h = call(numer_h_kernel, shape((2, N_CHIP * WIDE, TILE), f32), wide, [tiles, flip, halves])
+    numer_h = call(numer_h_kernel, (shape((N_CHIP * WIDE, TILE), f32),) * 2, wide, [tiles, flip, halves])
     update_h = call(update_h_kernel, (h_own, h_spread), [VMEM] * 2)
     numer_w = call(numer_w_kernel, shape((N_KMER * ROWS, TILE), f32), wide, [tiles, acc])
     update_w = call(update_w_kernel, (w_own, w_spread), [VMEM] * 2)
@@ -222,8 +222,8 @@
     w_panel = to_kmer(w_out)
     h_panel = panel_of(h_out)
     for sweep in range(ITERS):
-        numer = numer_h(*slots, values, w_panel, h_panel)
-        numer = numer[0] + lax.ppermute(numer[1], "samp", swap(1))
+        own, other = numer_h(*slots, values, w_panel, h_panel)
+        numer = own + lax.ppermute(other, "samp", swap(1))
         parts = to_chips(numer.reshape(N_CHIP, WIDE, 1, TILE)).reshape(N_CHIP * WIDE, TILE)
         h_own, h_out = update_h(parts, h_own)
         h_panel = panel_of(h_out)

time: 169 us -> 169 us (level)
  no operation moved by 1% of the time
where the time goes in v8:
time: 169 us; the launch traced here: 167 us
  blocking collectives  110 us (65%)
  starting transfers between devices  31.9 us (19%)
  waiting for transfers between devices  14.8 us (9%)
  Pallas kernels  6.23 us (4%)
  local copies, waits for them, and re-layouts  2.78 us (2%)
    all_to_all x4, blocking collectives, to_chips(): return lax.all_to_all(x, 'samp', 0, 0, axis_index_groups=CHIPS)  48.8 us
    all_to_all x3, blocking collectives, to_kmer(): return lax.all_to_all(x, 'kmer', 0, 0)  47.5 us
    all_to_all x1, starting transfers between devices, to_kmer(): return lax.all_to_all(x, 'kmer', 0, 0)  14.8 us
    all_gather x3, blocking collectives, panel_of(): lax.all_gather(to_chips(spread), 'samp', axis=0, axis_index_groups=CORES)  13.2 us
    ppermute x2, starting transfers between devices, body(): numer = own + lax.ppermute(other, 'samp', swap(1))  9.53 us
    all_to_all x1, starting transfers between devices, to_chips(): return lax.all_to_all(x, 'samp', 0, 0, axis_index_groups=CHIPS)  7.58 us
    all_to_all x1, waiting for transfers between devices, to_kmer(): return lax.all_to_all(x, 'kmer', 0, 0)  7.47 us
    all_to_all x1, waiting for transfers between devices, to_chips(): return lax.all_to_all(x, 'samp', 0, 0, axis_index_groups=CHIPS)  4.29 us
  transfers between devices with their start and end apart: 4, of which 4 were waited for; matrix products, arithmetic and copies ran while one was open for 0% of the time, Pallas kernels for 0%

profile of v8, /device:TPU:1, one launch (start us, length us, event | category | flops | bytes accessed | tf_op | source)
XLA Modules:
  0.0 166.8 jit_solution(17909842122348678414)
XLA Ops:
  0.6 0.7 copy-done.1
  1.4 0.7 shard_map.78
  2.1 7.6 %all-to-all-start.1 = ((bf16[16,64,128]{2,1,0:T(8,128)(2,1)}), bf16[16,64,128]{2,1,0:T(8,128)(2,1)S(1)}, u32[]{:S(2)}, u32[]{:S(2)}) async-start(bf16[16,64,128]{2,1,0:T(8,128)(2,1)} %shard_map.78), calls=%async_computation.1 | async-start | bytes 524288 | tf_op jit(solution)/shard_map/all_to_all | solution.py:183
  10.4 0.7 copy-done.3
  11.1 0.7 copy-done.4
  11.7 0.7 copy-done.5
  12.4 0.7 shard_map.77
  13.1 4.3 %all-to-all-done.1 = bf16[16,64,128]{2,1,0:T(8,128)(2,1)S(1)} async-done(((bf16[16,64,128]{2,1,0:T(8,128)(2,1)}), bf16[16,64,128]{2,1,0:T(8,128)(2,1)S(1)}, u32[]{:S(2)}, u32[]{:S(2)}) %all-to-all-start.1) | async-done | bytes 262176 | tf_op jit(solution)/shard_map/all_to_all | solution.py:183
  17.4 14.8 %all-to-all-start = ((bf16[16,16,128]{2,1,0:T(8,128)(2,1)}), bf16[16,16,128]{2,1,0:T(8,128)(2,1)S(1)}, u32[]{:S(2)}, u32[]{:S(2)}) async-start(bf16[16,16,128]{2,1,0:T(8,128)(2,1)} %get-tuple-element.18), calls=%async_computation | async-start | bytes 131072 | tf_op jit(solution)/shard_map/all_to_all | solution.py:179
  32.2 4.2 %all-gather = bf16[32,64,128]{2,1,0:T(8,128)(2,1)S(1)} all-gather(bf16[16,64,128]{2,1,0:T(8,128)(2,1)S(1)} %all-to-all-done.1), channel_id=2, replica_groups={{0,16},{32,48},{64,80},{96,112},{128,144},{160,176},{192,208},{224,240}..., dimensions={0}, use_global_device_ids=true | all-gather | bytes 786432 | tf_op jit(solution)/shard_map/all_gather | solution.py:187
  36.4 7.5 %all-to-all-done.w_ref = bf16[16,16,128]{2,1,0:T(8,128)(2,1)S(1)} async-done(((bf16[16,16,128]{2,1,0:T(8,128)(2,1)}), bf16[16,16,128]{2,1,0:T(8,128)(2,1)S(1)}, u32[]{:S(2)}, u32[]{:S(2)}) %all-to-all-start) | async-done | bytes 65568 | tf_op jit(solution)/shard_map/all_to_all | solution.py:179
  43.8 0.9 shard_map.79
  44.7 5.5 %collective-permute-start = (f32[1040,128]{1,0:T(8,128)S(1)}, f32[1040,128]{1,0:T(8,128)S(1)}, u32[]{:S(2)}, u32[]{:S(2)}) collective-permute-start(f32[1040,128]{1,0:T(8,128)S(1)} %get-tuple-element.20), channel_id=1, source_target_pairs={{0,16},{16,0},{32,48},{48,32},{64,80},{80,64},{96,112},{112,96},{1... | collective-permute-start | bytes 1597448 | tf_op jit(solution)/shard_map/ppermute | solution.py:226
  50.2 1.5 collective-permute-done
  51.7 0.1 add.6
  51.8 13.6 %all_to_all.45 = f32[16,65,1,128]{3,2,1,0:T(1,128)S(1)} all-to-all(f32[16,65,1,128]{3,2,1,0:T(1,128)S(1)} %bitcast.26), channel_id=1, replica_groups={{0,32,64,96,128,160,192,224,256,288,320,352,384,416,448,480},{16,48,80,..., dimensions={0} | all-to-all | bytes 1064960 | tf_op jit(solution)/shard_map/all_to_all | solution.py:183
  65.4 0.1 shard_map.80
  65.6 10.8 %all_to_all.46 = bf16[16,64,128]{2,1,0:T(8,128)(2,1)S(1)} all-to-all(bf16[16,64,128]{2,1,0:T(8,128)(2,1)S(1)} %get-tuple-element.21), channel_id=1, replica_groups={{0,32,64,96,128,160,192,224,256,288,320,352,384,416,448,480},{16,48,80,..., dimensions={0} | all-to-all | bytes 524288 | tf_op jit(solution)/shard_map/all_to_all | solution.py:183
  76.3 4.5 %all-gather.1 = bf16[32,64,128]{2,1,0:T(8,128)(2,1)S(1)} all-gather(bf16[16,64,128]{2,1,0:T(8,128)(2,1)S(1)} %all_to_all.46), channel_id=3, replica_groups={{0,16},{32,48},{64,80},{96,112},{128,144},{160,176},{192,208},{224,240}..., dimensions={0}, use_global_device_ids=true | all-gather | bytes 786432 | tf_op jit(solution)/shard_map/all_gather | solution.py:187
  80.8 1.0 shard_map.81
  81.9 14.7 %all_to_all.47 = f32[16,17,1,128]{3,2,1,0:T(1,128)S(1)} all-to-all(f32[16,17,1,128]{3,2,1,0:T(1,128)S(1)} %bitcast.25), channel_id=1, replica_groups=mesh['samp'=32,'kmer'=16] {'kmer'}, dimensions={0} | all-to-all | bytes 278528 | tf_op jit(solution)/shard_map/all_to_all | solution.py:179
  96.6 18.1 %all_to_all.48.w_ref = bf16[16,16,128]{2,1,0:T(8,128)(2,1)S(1)} all-to-all(bf16[16,16,128]{2,1,0:T(8,128)(2,1)S(1)} %get-tuple-element.23), channel_id=1, replica_groups=mesh['samp'=32,'kmer'=16] {'kmer'}, dimensions={0} | all-to-all | bytes 131072 | tf_op jit(solution)/shard_map/all_to_all | solution.py:179
  114.7 0.9 shard_map.83
  115.6 4.1 %collective-permute-start.1 = (f32[1040,128]{1,0:T(8,128)S(1)}, f32[1040,128]{1,0:T(8,128)S(1)}, u32[]{:S(2)}, u32[]{:S(2)}) collective-permute-start(f32[1040,128]{1,0:T(8,128)S(1)} %get-tuple-element.25), channel_id=1, source_target_pairs={{0,16},{16,0},{32,48},{48,32},{64,80},{80,64},{96,112},{112,96},{1... | collective-permute-start | bytes 1597448 | tf_op jit(solution)/shard_map/ppermute | solution.py:226
  119.6 1.5 collective-permute-done.1
  121.2 13.6 %all_to_all.49 = f32[16,65,1,128]{3,2,1,0:T(1,128)S(1)} all-to-all(f32[16,65,1,128]{3,2,1,0:T(1,128)S(1)} %bitcast.27), channel_id=1, replica_groups={{0,32,64,96,128,160,192,224,256,288,320,352,384,416,448,480},{16,48,80,..., dimensions={0} | all-to-all | bytes 1064960 | tf_op jit(solution)/shard_map/all_to_all | solution.py:183
  134.9 0.1 shard_map.84
  135.0 10.8 %all_to_all.50 = bf16[16,64,128]{2,1,0:T(8,128)(2,1)S(1)} all-to-all(bf16[16,64,128]{2,1,0:T(8,128)(2,1)S(1)} %get-tuple-element.27), channel_id=1, replica_groups={{0,32,64,96,128,160,192,224,256,288,320,352,384,416,448,480},{16,48,80,..., dimensions={0} | all-to-all | bytes 524288 | tf_op jit(solution)/shard_map/all_to_all | solution.py:183
  145.7 4.5 %all-gather.2 = bf16[32,64,128]{2,1,0:T(8,128)(2,1)S(1)} all-gather(bf16[16,64,128]{2,1,0:T(8,128)(2,1)S(1)} %all_to_all.50), channel_id=4, replica_groups={{0,16},{32,48},{64,80},{96,112},{128,144},{160,176},{192,208},{224,240}..., dimensions={0}, use_global_device_ids=true | all-gather | bytes 786432 | tf_op jit(solution)/shard_map/all_gather | solution.py:187
  150.3 1.0 shard_map.85
  151.3 14.8 %all_to_all.51 = f32[16,17,1,128]{3,2,1,0:T(1,128)S(1)} all-to-all(f32[16,17,1,128]{3,2,1,0:T(1,128)S(1)} %bitcast.24), channel_id=1, replica_groups=mesh['samp'=32,'kmer'=16] {'kmer'}, dimensions={0} | all-to-all | bytes 278528 | tf_op jit(solution)/shard_map/all_to_all | solution.py:179
  166.1 0.7 shard_map.86
  (10 shorter events, 0.1 us)
Async XLA Ops:
  0.6 0.8 copy-start.1
  1.4 42.4 %copy-start = (bf16[1,1,32,128,128]{4,3,2,1,0:T(8,128)(2,1)S(1)}, bf16[1,1,32,128,128]{4,3,2,1,0:T(8,128)(2,1)}, u32[]{:S(2)}) copy-start(bf16[1,1,32,128,128]{4,3,2,1,0:T(8,128)(2,1)} %param.9) | copy-start | bytes 3145732
  2.1 15.3 %all-to-all-start.1 = ((bf16[16,64,128]{2,1,0:T(8,128)(2,1)}), bf16[16,64,128]{2,1,0:T(8,128)(2,1)S(1)}, u32[]{:S(2)}, u32[]{:S(2)}) async-start(bf16[16,64,128]{2,1,0:T(8,128)(2,1)} %shard_map.78), calls=%async_computation.1 | async-start | bytes 524288 | tf_op jit(solution)/shard_map/all_to_all | solution.py:183
  10.4 0.7 copy-start.3
  11.1 0.7 copy-start.4
  11.7 0.7 copy-start.5
  17.4 26.5 %all-to-all-start = ((bf16[16,16,128]{2,1,0:T(8,128)(2,1)}), bf16[16,16,128]{2,1,0:T(8,128)(2,1)S(1)}, u32[]{:S(2)}, u32[]{:S(2)}) async-start(bf16[16,16,128]{2,1,0:T(8,128)(2,1)} %get-tuple-element.18), calls=%async_computation | async-start | bytes 131072 | tf_op jit(solution)/shard_map/all_to_all | solution.py:179
  44.7 7.0 %collective-permute-start = (f32[1040,128]{1,0:T(8,128)S(1)}, f32[1040,128]{1,0:T(8,128)S(1)}, u32[]{:S(2)}, u32[]{:S(2)}) collective-permute-start(f32[1040,128]{1,0:T(8,128)S(1)} %get-tuple-element.20), channel_id=1, source_target_pairs={{0,16},{16,0},{32,48},{48,32},{64,80},{80,64},{96,112},{112,96},{1... | collective-permute-start | bytes 1597448 | tf_op jit(solution)/shard_map/ppermute | solution.py:226
  51.8 13.6 %copy-start.2 = (f32[64,128]{1,0:T(8,128)S(1)}, f32[64,128]{1,0:T(8,128)}, u32[]{:S(2)}) copy-start(f32[64,128]{1,0:T(8,128)} %h_ref.3) | copy-start | bytes 98308
  115.6 5.6 %collective-permute-start.1 = (f32[1040,128]{1,0:T(8,128)S(1)}, f32[1040,128]{1,0:T(8,128)S(1)}, u32[]{:S(2)}, u32[]{:S(2)}) collective-permute-start(f32[1040,128]{1,0:T(8,128)S(1)} %get-tuple-element.25), channel_id=1, source_target_pairs={{0,16},{16,0},{32,48},{48,32},{64,80},{80,64},{96,112},{112,96},{1... | collective-permute-start | bytes 1597448 | tf_op jit(solution)/shard_map/ppermute | solution.py:226
